TPU v7x, 128 devices: a whole 4x4x4 slice. The times are simulated.
128 devices in a mesh: section: 4 (over x), dp: 16 (over z, y), tensor: 2 (over core).
Axes of the slice: x: 4, y: 4, z: 4, core: 2. Of those that a mesh axis runs over, the one named last changes fastest.
Arguments:
- latent_states: bfloat16 [4, 16, 512, 1, 5120], P('section', 'dp', 'tensor'), may hold values from -6 to 6
- piece_extents: int32 [4, 16, 1, 4], P('section', 'dp'), may hold values from 1 to 256, 512 in all within a row
- retained_bundles: int32 [3, 16], replicated, may hold values from -1 to 15, as said below
- mixer_scaling_factor: bfloat16 [4, 5120], P('section'), may hold values from 0.099609375 to 1.8984375
- asker_projector: bfloat16 [4, 5120, 3072], P('section', None, 'tensor')
- asker_offset_vector: bfloat16 [4, 3072], P('section', 'tensor'), may hold values from -3 to 3
- lookup_projector: bfloat16 [4, 5120, 1024], P('section', None, 'tensor'), may hold values from -0.078125 to 0.078125
- content_projector: bfloat16 [4, 5120, 1024], P('section', None, 'tensor'), may hold values from -0.078125 to 0.078125
- content_offset_vector: bfloat16 [4, 1024], P('section', 'tensor'), may hold values from -3 to 3
- mixer_output_matrix: bfloat16 [4, 3072, 5120], P('section', 'tensor'), may hold values from -0.109375 to 0.109375
- leave_rating_matrix: bfloat16 [4, 5120], P('section'), may hold values from -0.078125 to 0.078125
Outputs:
- scores: float32 [4, 16, 1, 4], P('section', 'dp')
- next_hidden: bfloat16 [4, 16, 512, 1, 5120], P('section', 'dp', 'tensor')
Inputs may be any that keep to these rules, and one draw needn't show every extreme that they name: retained_bundles[s] lists in increasing order the numbers of the packs of phase s that pass its exit, then -1 entries; its k-th entry fills the pack numbered k of phase s + 1.
All inputs are finite; a program needn't handle non-finite values.
Results may differ from a plain program's by a relative error of at most 0.013.
The roundings to bfloat16 on the way count: a program that leaves them out, or rounds other values in their place, can miss the bound.
Values may be sent and summed in bfloat16 or wider, within the bound.
No kernel may reach another device: no remote copies, remote signals or barrier semaphores. Data moves between devices by JAX's collectives and lax.ppermute only.
A program may use at most 256 MiB of HBM per device.

v0:
```python
import jax
import jax.numpy as jnp
from jax import lax
from jax.sharding import PartitionSpec as P

HD = 128


epsilon = 1e-06
rope_base = 1000000.0


def passed_along(value, axis, steps):
    count = lax.axis_size(axis)
    leading, last = (max(0, -steps), min(count, count - steps))
    return lax.ppermute(value, axis, [(source, source + steps) for source in range(leading, last)])


def segment_layout(lengths, length):
    ends = jnp.cumsum(lengths, axis=-1)
    starts = ends - lengths
    places = jnp.arange(length, dtype=jnp.int32)
    segment = jnp.sum((places[:, None] >= ends[..., None, :]).astype(jnp.int32), axis=-1)
    member = (segment[..., None] == jnp.arange(lengths.shape[-1], dtype=jnp.int32)).astype(
        jnp.int32
    )
    offset = places - jnp.sum(member * starts[..., None, :], axis=-1)
    return (segment, offset, ends - 1)


def rotate(vectors, angle):
    half = vectors.shape[-1] // 2
    first = vectors[..., :half]
    second = vectors[..., half:]
    cosine = jnp.cos(angle)
    sine = jnp.sin(angle)
    return jnp.concatenate(
        [first * cosine - second * sine, second * cosine + first * sine], axis=-1
    )


def frequencies(width):
    return jnp.exp(-jnp.log(rope_base) * jnp.arange(0, width, 2, dtype=jnp.float32) / width)


def row_norm(vectors):
    return vectors * lax.rsqrt(jnp.mean(vectors * vectors, axis=-1, keepdims=True) + epsilon)


def on_device(
    latent_states,
    piece_extents,
    retained_bundles,
    mixer_scaling_factor,
    asker_projector,
    asker_offset_vector,
    lookup_projector,
    content_projector,
    content_offset_vector,
    mixer_output_matrix,
    leave_rating_matrix,
):
    local_rows = latent_states[0, 0]
    rows_here = local_rows.shape[0]
    openings = local_rows.shape[1]
    pair_len = rows_here * lax.axis_size("tensor")
    hidden_f = local_rows.astype(jnp.float32)
    normed = (row_norm(hidden_f) * mixer_scaling_factor[0].astype(jnp.float32)).astype(jnp.bfloat16)
    w_query = asker_projector[0]
    w_key = lookup_projector[0]
    w_value = content_projector[0]
    q_width = w_query.shape[1]
    k_width = w_key.shape[1]
    kv_here = k_width // HD
    q_group = q_width // k_width
    q_shift = asker_offset_vector[0].astype(jnp.float32)
    v_shift = content_offset_vector[0].astype(jnp.float32)
    piece = lax.all_gather(normed, "tensor", axis=0, tiled=True)
    query_part = (
        jnp.einsum("rsd,dc->rsc", piece, w_query, preferred_element_type=jnp.float32) + q_shift
    )
    key_part = jnp.einsum("rsd,dc->rsc", piece, w_key, preferred_element_type=jnp.float32)
    value_part = (
        jnp.einsum("rsd,dc->rsc", piece, w_value, preferred_element_type=jnp.float32) + v_shift
    )
    joined = jnp.concatenate([query_part, key_part, value_part], axis=2)
    segment, offset, last = segment_layout(piece_extents[0, 0], pair_len)
    angle = offset.astype(jnp.float32)[..., None] * frequencies(HD)
    angle = jnp.swapaxes(angle, 0, 1)
    query = joined[..., :q_width].reshape(pair_len, openings, kv_here, q_group, HD)
    query = rotate(query, angle[:, :, None, None, :]).astype(jnp.bfloat16)
    keys = joined[..., q_width : q_width + k_width].reshape(pair_len, openings, kv_here, HD)
    keys = rotate(keys, angle[:, :, None, :]).astype(jnp.bfloat16)
    values = (
        joined[..., q_width + k_width :]
        .astype(jnp.bfloat16)
        .reshape(pair_len, openings, kv_here, HD)
    )
    logits = jnp.einsum(
        "qsgph,ksgh->sgpqk", query, keys, preferred_element_type=jnp.float32
    ) * HD ** (-0.5)
    places = jnp.arange(pair_len, dtype=jnp.int32)
    allowed = (segment[:, :, None] == segment[:, None, :]) & (
        places[None, None, :] <= places[None, :, None]
    )
    logits = jnp.where(allowed[:, None, None], logits, -1e30)
    peak = jnp.max(logits, axis=-1, keepdims=True)
    expons = jnp.exp(logits - peak)
    probs = (expons / jnp.sum(expons, axis=-1, keepdims=True)).astype(jnp.bfloat16)
    mixed = jnp.einsum("sgpqk,ksgh->qsgph", probs, values, preferred_element_type=jnp.float32)
    mixed = mixed.astype(jnp.bfloat16).reshape(pair_len, openings, q_width)
    w_out = mixer_output_matrix[0]
    piece = mixed
    branch = lax.psum_scatter(
        jnp.einsum("rsc,cd->rsd", piece, w_out, preferred_element_type=jnp.float32).astype(
            jnp.bfloat16
        ),
        "tensor",
        scatter_dimension=0,
        tiled=True,
    ).astype(jnp.float32)
    summed = hidden_f + branch
    phase_out = summed.astype(jnp.bfloat16)
    row_scores = jnp.sum(row_norm(summed) * leave_rating_matrix[0].astype(jnp.float32), axis=-1)
    global_rows = lax.axis_index("tensor") * rows_here + jnp.arange(rows_here, dtype=jnp.int32)
    picked = global_rows[:, None, None] == last[None, :, :]
    partial_scores = jnp.sum(jnp.where(picked, row_scores[:, :, None], 0.0), axis=0)
    seg_scores = lax.psum(partial_scores, "tensor")
    active_round_ordinal = lax.axis_index("section")
    cluster_ordinal = lax.axis_index("dp")
    moved = passed_along(phase_out, "section", 1)
    keeper_catalog = lax.dynamic_index_in_dim(
        retained_bundles, jnp.maximum(active_round_ordinal - 1, 0), 0, keepdims=False
    )
    demanded_lines = lax.dynamic_slice_in_dim(keeper_catalog, cluster_ordinal * openings, openings)
    everyone = lax.all_gather(moved, "dp", axis=1, tiled=True)
    chosen = jnp.take(everyone, jnp.maximum(demanded_lines, 0), axis=1)
    arrived = jnp.where((demanded_lines >= 0)[None, :, None], chosen, jnp.zeros_like(chosen))
    return (seg_scores[None, None], arrived[None, None])


def solution(mesh):
    return jax.shard_map(
        on_device,
        mesh=mesh,
        in_specs=(
            P("section", "dp", "tensor", None, None),
            P("section", "dp", None, None),
            P(),
            P("section", None),
            P("section", None, "tensor"),
            P("section", "tensor"),
            P("section", None, "tensor"),
            P("section", None, "tensor"),
            P("section", "tensor"),
            P("section", "tensor", None),
            P("section", None),
        ),
        out_specs=(P("section", "dp", None, None), P("section", "dp", "tensor", None, None)),
        check_vma=False,
    )
```

profile of v0, /device:TPU:2, one launch (start us, length us, event | category | flops | bytes accessed | tf_op | source)
XLA Modules:
  0.0 433.7 jit_solution(14405912064260780205)
XLA Ops:
  7.2 0.8 convert_element_type.153
  8.0 2.3 fusion.15
  10.3 4.0 fusion.17
  14.8 0.5 multiply_cosine_fusion
  15.4 0.8 copy.41
  16.2 0.8 copy.39
  17.1 7.9 %copy.47 = bf16[512,5120]{1,0:T(8,128)(2,1)} copy(bf16[512,5120]{0,1:T(8,128)(2,1)} %bitcast.115) | data formatting | bytes 10485760 | tf_op jit(solution)/shard_map/reshape.267
  25.0 0.2 fusion.52
  25.2 9.7 %all-gather.3.cloned.1.call-done = bf16[512,1,5120]{2,0,1:T(8,128)(2,1)} async-done(((bf16[256,1,5120]{2,0,1:T(8,128)(2,1)}), bf16[512,1,5120]{2,0,1:T(8,128)(2,1)}) %all-gather.3.cloned.1.call-update) | async-done | bytes 5242896 | tf_op jit(solution)/shard_map/all_gather | solution.py:78
  34.9 14.4 %fusion.25 = f32[512,1536]{1,0:T(8,128)} fusion(bf16[1,5120,1536]{2,1,0:T(8,128)(2,1)} %param.15, bf16[512,1,5120]{2,0,1:T(8,128)(2,1)} %all-gather.3.cloned.1.call-done, f32[1536]{0:T(1024)S(1)} %convert_reduce_fusion.1), kind=kOutput, calls=%fused_computation.29 | convolution fusion | flops 8053850112 | bytes 24123392 | tf_op jit(solution)/shard_map/rsd,dc->rsc/dot_general | solution.py:80
  49.3 2.4 copy.37
  51.7 2.1 fusion.60
  53.8 2.1 copy.51
  55.9 3.4 copy.50
  59.3 6.8 %fusion.39 = f32[512,1,4,128]{0,3,2,1:T(8,128)S(1)} fusion(bf16[4,128,5120]{2,1,0:T(8,128)(2,1)} %bitcast.116, bf16[512,1,5120]{2,0,1:T(8,128)(2,1)} %all-gather.3.cloned.1.call-done), kind=kOutput, calls=%fused_computation.40 | convolution fusion | flops 2684354560 | bytes 11534336 | tf_op jit(solution)/shard_map/rsd,dc->rsc/dot_general | solution.py:82
  66.3 0.9 fusion.33
  67.2 3.6 fusion.5
  70.7 2.6 fusion.4
  73.4 7.0 %fusion.47 = bf16[512,512]{0,1:T(8,128)(2,1)S(1)} fusion(bf16[1,5120,512]{2,1,0:T(8,128)(2,1)} %param.18, bf16[512,1,5120]{2,0,1:T(8,128)(2,1)} %all-gather.3.cloned.1.call-done, f32[512]{0:T(512)S(1)} %bitcast.119), kind=kOutput, calls=%fused_computation.42 | convolution fusion | flops 2684878848 | bytes 11012096 | tf_op jit(solution)/shard_map/rsd,dc->rsc/dot_general | solution.py:84
  80.3 3.9 fusion.30
  84.2 13.7 %fusion.9 = bf16[512,1,5120]{2,0,1:T(8,128)(2,1)} fusion(bf16[512,1536]{0,1:T(8,128)(2,1)S(1)} %bitcast.123, bf16[1,1536,5120]{2,1,0:T(8,128)(2,1)} %param.20), kind=kOutput, calls=%fused_computation.13 | convolution fusion | flops 8055685120 | bytes 22544384 | tf_op jit(solution)/shard_map/rsc,cd->rsd/dot_general | solution.py:115
  98.0 0.6 copy-done.8
  98.6 16.8 %reduce-scatter.2.cloned.1.call-done = bf16[256,1,5120]{2,0,1:T(8,128)(2,1)} async-done(((bf16[512,1,5120]{2,0,1:T(8,128)(2,1)}), bf16[256,1,5120]{2,0,1:T(8,128)(2,1)}) %reduce-scatter.2.cloned.1.call-update) | async-done | bytes 2621456 | tf_op jit(solution)/shard_map/reduce_scatter | solution.py:114
  115.4 2.8 multiply_reduce_fusion.1
  118.2 1.4 fusion.24
  119.7 3.4 collective-permute-start
  123.1 57.5 %collective-permute-done = bf16[256,1,5120]{2,0,1:T(8,128)(2,1)S(1)} collective-permute-done((bf16[256,1,5120]{2,0,1:T(8,128)(2,1)S(1)}, bf16[256,1,5120]{2,0,1:T(8,128)(2,1)S(1)}, u32[]{:S(2)}, u32[]{:S(2)}) %collective-permute-start) | collective-permute-done | bytes 2621472 | tf_op jit(solution)/shard_map/ppermute | solution.py:16
  180.6 1.5 copy-done.3
  182.1 1.3 dynamic_slice.5
  184.9 3.0 psum.7
  187.9 235.8 %all-gather.5.cloned.1.call-done = bf16[256,16,5120]{2,0,1:T(8,128)(2,1)} async-done(((bf16[256,1,5120]{2,0,1:T(8,128)(2,1)}), bf16[256,16,5120]{2,0,1:T(8,128)(2,1)}) %all-gather.5.cloned.1.call-update) | async-done | bytes 41943056 | tf_op jit(solution)/shard_map/all_gather | solution.py:136
  423.6 3.5 select_bitcast_fusion
  (42 shorter events, 1.0 us)
Async XLA Ops:
  7.2 27.7 %all-gather.3.cloned.1.call-start = ((), (), s32[]{:S(2)}) async-start(), calls=%async_computation.1 | async-start | bytes 7864320 | tf_op jit(solution)/shard_map/all_gather | solution.py:78
  8.0 6.5 %copy-start.10 = (bf16[1,512]{1,0:T(2,128)(2,1)S(1)}, bf16[1,512]{1,0:T(2,128)(2,1)}, u32[]{:S(2)}) copy-start(bf16[1,512]{1,0:T(2,128)(2,1)} %param.19) | copy-start | bytes 3076
  8.0 6.5 %copy-start.11 = (s32[1,1,1,4]{3,2,1,0:T(1,128)S(1)}, s32[1,1,1,4]{3,2,1,0:T(1,128)}, u32[]{:S(2)}) copy-start(s32[1,1,1,4]{3,2,1,0:T(1,128)} %param.12) | copy-start | bytes 52
  14.4 101.0 %reduce-scatter.2.cloned.1.call-start = ((), (), s32[]{:S(2)}) async-start(), calls=%async_computation.2 | async-start | bytes 7864320 | tf_op jit(solution)/shard_map/reduce_scatter | solution.py:114
  15.4 9.6 %copy-start.4 = (f32[512,64]{0,1:T(8,128)}, f32[512,64]{0,1:T(8,128)S(1)}, u32[]{:S(2)}) copy-start(f32[512,64]{0,1:T(8,128)S(1)} %get-tuple-element.22) | copy-start | bytes 393220
  17.1 7.9 %copy-start.9 = (bf16[1,1536]{1,0:T(2,128)(2,1)S(1)}, bf16[1,1536]{1,0:T(2,128)(2,1)}, u32[]{:S(2)}) copy-start(bf16[1,1536]{1,0:T(2,128)(2,1)} %param.16) | copy-start | bytes 9220
  59.3 6.8 %copy-start.5 = (f32[512,64]{0,1:T(8,128)S(1)}, f32[512,64]{0,1:T(8,128)}, u32[]{:S(2)}) copy-start(f32[512,64]{0,1:T(8,128)} %copy-done.4) | copy-start | bytes 393220
  59.3 7.0 %copy-start.1 = (f32[512,1,4,3,64]{4,0,3,2,1:T(8,128)S(1)}, f32[512,1,4,3,64]{4,0,3,2,1:T(8,128)}, u32[]{:S(2)}) copy-start(f32[512,1,4,3,64]{4,0,3,2,1:T(8,128)} %copy.50) | copy-start | bytes 4718596
  59.3 7.0 %copy-start.6 = (f32[512,64]{1,0:T(8,128)S(1)}, f32[512,64]{1,0:T(8,128)}, u32[]{:S(2)}) copy-start(f32[512,64]{1,0:T(8,128)} %copy.41) | copy-start | bytes 393220
  59.3 7.0 %copy-start.7 = (f32[512,64]{1,0:T(8,128)S(1)}, f32[512,64]{1,0:T(8,128)}, u32[]{:S(2)}) copy-start(f32[512,64]{1,0:T(8,128)} %copy.39) | copy-start | bytes 393220
  97.9 0.7 copy-start.8
  97.9 17.5 %copy-start = (bf16[1,1,256,1,5120]{4,2,3,1,0:T(8,128)(2,1)S(1)}, bf16[1,1,256,1,5120]{4,2,3,1,0:T(8,128)(2,1)}, u32[]{:S(2)}) copy-start(bf16[1,1,256,1,5120]{4,2,3,1,0:T(8,128)(2,1)} %param.11) | copy-start | bytes 7864324
  97.9 325.7 %all-gather.5.cloned.1.call-start = ((), (), s32[]{:S(2)}) async-start(), calls=%async_computation.3 | async-start | bytes 44564480 | tf_op jit(solution)/shard_map/all_gather | solution.py:136
  115.4 2.8 copy-start.2
  119.7 60.9 %collective-permute-start = (bf16[256,1,5120]{2,0,1:T(8,128)(2,1)S(1)}, bf16[256,1,5120]{2,0,1:T(8,128)(2,1)S(1)}, u32[]{:S(2)}, u32[]{:S(2)}) collective-permute-start(bf16[256,1,5120]{2,0,1:T(8,128)(2,1)S(1)} %get-tuple-element.15), channel_id=1, source_target_pairs={{0,32},{32,64},{64,96},{1,33},{33,65},{65,97},{2,34},{34,66},{66,9... | collective-permute-start | bytes 7864328 | tf_op jit(solution)/shard_map/ppermute | solution.py:16
  180.6 1.5 copy-start.3
Sparse Core Ops, SparseCore 0:
  14.5 20.3 all-gather.2
  98.0 17.3 reduce-scatter.1
  182.2 241.3 all-gather.4
where the time goes:
time: 435 us; the launch traced here: 434 us
  waiting for transfers between devices  320 us (74%)
  matrix products  49.3 us (11%)
  local copies, waits for them, and re-layouts  22.9 us (5%)
  other arithmetic  19.9 us (5%)
  between operations  15.3 us (4%)
    all_gather x1, waiting for transfers between devices, on_device(): everyone = lax.all_gather(moved, 'dp', axis=1, tiled=True)  236 us
    ppermute x1, waiting for transfers between devices, passed_along(): lax.ppermute(value, axis, [(source, source + steps) for source in range(l...  57.5 us
    reduce_scatter x1, waiting for transfers between devices, on_device(): lax.psum_scatter(jnp.einsum('rsc,cd->rsd', piece, w_out, preferred_elemen...  16.8 us
    dot_general x1, matrix products, on_device(): jnp.einsum('rsd,dc->rsc', piece, w_query, preferred_element_type=jnp.floa...  14.4 us
    dot_general x1, matrix products, on_device(): jnp.einsum('rsc,cd->rsd', piece, w_out, preferred_element_type=jnp.float32)  13.7 us
    all_gather x1, waiting for transfers between devices, on_device(): piece = lax.all_gather(normed, 'tensor', axis=0, tiled=True)  9.71 us
  transfers between devices with their start and end apart: 4, of which 4 were waited for; matrix products, arithmetic and copies ran while one was open for 3% of the time, Pallas kernels for 0%

commit v1 on v0

v1 whole, which is shorter than its diff:
```python
import jax
import jax.numpy as jnp
from jax import lax
from jax.sharding import PartitionSpec as P

HD = 128
CHUNKS = 2


epsilon = 1e-06
rope_base = 1000000.0


def segment_layout(lengths, length):
    ends = jnp.cumsum(lengths, axis=-1)
    starts = ends - lengths
    places = jnp.arange(length, dtype=jnp.int32)
    segment = jnp.sum((places[:, None] >= ends[..., None, :]).astype(jnp.int32), axis=-1)
    member = (segment[..., None] == jnp.arange(lengths.shape[-1], dtype=jnp.int32)).astype(
        jnp.int32
    )
    offset = places - jnp.sum(member * starts[..., None, :], axis=-1)
    return (segment, offset, ends - 1)


def rotate(vectors, angle):
    half = vectors.shape[-1] // 2
    first = vectors[..., :half]
    second = vectors[..., half:]
    cosine = jnp.cos(angle)
    sine = jnp.sin(angle)
    return jnp.concatenate(
        [first * cosine - second * sine, second * cosine + first * sine], axis=-1
    )


def frequencies(width):
    return jnp.exp(-jnp.log(rope_base) * jnp.arange(0, width, 2, dtype=jnp.float32) / width)


def row_norm(vectors):
    return vectors * lax.rsqrt(jnp.mean(vectors * vectors, axis=-1, keepdims=True) + epsilon)


def swap(value):
    return lax.ppermute(value, "tensor", [(0, 1), (1, 0)])


def on_device(
    latent_states,
    piece_extents,
    retained_bundles,
    mixer_scaling_factor,
    asker_projector,
    asker_offset_vector,
    lookup_projector,
    content_projector,
    content_offset_vector,
    mixer_output_matrix,
    leave_rating_matrix,
):
    local = latent_states[0, 0, :, 0]
    rows, width = local.shape
    tensor = lax.axis_index("tensor")
    section = lax.axis_index("section")
    n_dp = lax.axis_size("dp")
    pair_len = rows * 2
    hidden_f = local.astype(jnp.float32)
    normed = (row_norm(hidden_f) * mixer_scaling_factor[0].astype(jnp.float32)).astype(jnp.bfloat16)
    w_query = asker_projector[0]
    w_key = lookup_projector[0]
    w_value = content_projector[0]
    q_width = w_query.shape[1]
    k_width = w_key.shape[1]
    kv_here = k_width // HD
    q_group = q_width // k_width
    q_shift = asker_offset_vector[0].astype(jnp.float32)
    v_shift = content_offset_vector[0].astype(jnp.float32)
    other = swap(normed)
    first = jnp.where(tensor == 0, normed, other)
    second = jnp.where(tensor == 0, other, normed)
    piece = jnp.concatenate([first, second], axis=0)
    query = jnp.dot(piece, w_query, preferred_element_type=jnp.float32) + q_shift
    keys = jnp.dot(piece, w_key, preferred_element_type=jnp.float32)
    values = (jnp.dot(piece, w_value, preferred_element_type=jnp.float32) + v_shift).astype(
        jnp.bfloat16
    )
    segment, offset, last = segment_layout(piece_extents[0, 0, 0], pair_len)
    angle = offset.astype(jnp.float32)[:, None] * frequencies(HD)
    query = rotate(query.reshape(pair_len, kv_here, q_group, HD), angle[:, None, None, :])
    query = query.astype(jnp.bfloat16)
    keys = rotate(keys.reshape(pair_len, kv_here, HD), angle[:, None, :]).astype(jnp.bfloat16)
    values = values.reshape(pair_len, kv_here, HD)
    logits = jnp.einsum(
        "qgph,kgh->gpqk", query, keys, preferred_element_type=jnp.float32
    ) * HD ** (-0.5)
    places = jnp.arange(pair_len, dtype=jnp.int32)
    allowed = (segment[:, None] == segment[None, :]) & (places[None, :] <= places[:, None])
    logits = jnp.where(allowed, logits, -1e30)
    peak = jnp.max(logits, axis=-1, keepdims=True)
    expons = jnp.exp(logits - peak)
    probs = (expons / jnp.sum(expons, axis=-1, keepdims=True)).astype(jnp.bfloat16)
    mixed = jnp.einsum("gpqk,kgh->qgph", probs, values, preferred_element_type=jnp.float32)
    mixed = mixed.astype(jnp.bfloat16).reshape(pair_len, q_width)
    w_out = mixer_output_matrix[0]
    rating = leave_rating_matrix[0].astype(jnp.float32)

    wanted = lax.dynamic_index_in_dim(
        retained_bundles, jnp.minimum(section, retained_bundles.shape[0] - 1), 0, keepdims=False
    )
    forward = [(s, s + 1) for s in range(lax.axis_size("section") - 1)]
    step = width // CHUNKS
    squares = 0.0
    graded = 0.0
    arrived = []
    for c in range(CHUNKS):
        span = slice(c * step, (c + 1) * step)
        term = jnp.dot(mixed, w_out[:, span], preferred_element_type=jnp.float32).astype(
            jnp.bfloat16
        )
        mine = lax.dynamic_slice_in_dim(term, tensor * rows, rows, 0)
        theirs = lax.dynamic_slice_in_dim(term, (1 - tensor) * rows, rows, 0)
        received = swap(theirs)
        summed = hidden_f[:, span] + (mine.astype(jnp.float32) + received.astype(jnp.float32))
        squares = squares + jnp.sum(summed * summed, axis=-1)
        graded = graded + jnp.sum(summed * rating[span], axis=-1)
        out = summed.astype(jnp.bfloat16).reshape(n_dp, rows // n_dp, step)
        spread = lax.all_to_all(out, "dp", 0, 0)
        chosen = jnp.take(spread, jnp.maximum(wanted, 0), axis=0)
        chosen = jnp.where((wanted >= 0)[:, None, None], chosen, jnp.zeros_like(chosen))
        moved = lax.ppermute(chosen, "section", forward)
        arrived.append(lax.all_to_all(moved, "dp", 0, 0).reshape(rows, step))
    row_scores = graded * lax.rsqrt(squares / width + epsilon)
    global_rows = tensor * rows + jnp.arange(rows, dtype=jnp.int32)
    picked = global_rows[:, None] == last[None, :]
    partial_scores = jnp.sum(jnp.where(picked, row_scores[:, None], 0.0), axis=0)
    seg_scores = lax.psum(partial_scores, "tensor")
    arrived = jnp.concatenate(arrived, axis=1)
    return (seg_scores[None, None, None], arrived[None, None, :, None, :])


def solution(mesh):
    return jax.shard_map(
        on_device,
        mesh=mesh,
        in_specs=(
            P("section", "dp", "tensor", None, None),
            P("section", "dp", None, None),
            P(),
            P("section", None),
            P("section", None, "tensor"),
            P("section", "tensor"),
            P("section", None, "tensor"),
            P("section", None, "tensor"),
            P("section", "tensor"),
            P("section", "tensor", None),
            P("section", None),
        ),
        out_specs=(P("section", "dp", None, None), P("section", "dp", "tensor", None, None)),
        check_vma=False,
    )
```

time: 435 us -> 249 us (0.57)
  waiting for transfers between devices: 320 us -> 81.8 us
  blocking collectives: 2.97 us -> 31.6 us
  starting transfers between devices: 3.5 us -> 20.9 us
  between operations: 15.3 us -> 1.07 us
  other arithmetic: 19.9 us -> 33 us
  local copies, waits for them, and re-layouts: 22.9 us -> 32.5 us
    all_gather x2 -> x0, waiting for transfers between devices: 245 us -> none  [the longest x1 236 us: on_device(): everyone = lax.all_gather(moved, 'dp', axis=1, tiled=True)]
    all_to_all x0 -> x3, waiting for transfers between devices: none -> 31.1 us  [the longest x1 17.3 us: on_device(): spread = lax.all_to_all(out, 'dp', 0, 0)]
    all_to_all x0 -> x1, blocking collectives: none -> 28.6 us  [on_device(): spread = lax.all_to_all(out, 'dp', 0, 0)]
    reduce_scatter x1 -> x0, waiting for transfers between devices: 16.8 us -> none  [on_device(): lax.psum_scatter(jnp.einsum('rsc,cd->rsd', piece, w_out, preferred_elemen...]
    all_to_all x0 -> x3, starting transfers between devices: none -> 13.7 us  [the longest x2 9.34 us: on_device(): arrived.append(lax.all_to_all(moved, 'dp', 0, 0).reshape(rows, step))]
    sub x0 -> x1, other arithmetic: none -> 8.21 us  [on_device(): expons = jnp.exp(logits - peak)]
    dot_general x0 -> x1, local copies, waits for them, and re-layouts: none -> 7.88 us  [on_device(): keys = jnp.dot(piece, w_key, preferred_element_type=jnp.float32)]
    another operation x1 -> x0, local copies, waits for them, and re-layouts: 7.87 us -> none
  transfers between devices with their start and end apart: 4 -> 8, of which waited for: 4 -> 6; matrix products, arithmetic and copies ran while one was open for 3% -> 7% of each run, Pallas kernels for 0% -> 0%
where the time goes in v1:
time: 249 us; the launch traced here: 248 us
  waiting for transfers between devices  81.8 us (33%)
  matrix products  47.5 us (19%)
  other arithmetic  33 us (13%)
  local copies, waits for them, and re-layouts  32.5 us (13%)
  blocking collectives  31.6 us (13%)
  starting transfers between devices  20.9 us (8%)
    ppermute x2, waiting for transfers between devices, on_device(): moved = lax.ppermute(chosen, 'section', forward)  47 us
    all_to_all x1, blocking collectives, on_device(): spread = lax.all_to_all(out, 'dp', 0, 0)  28.6 us
    all_to_all x1, waiting for transfers between devices, on_device(): spread = lax.all_to_all(out, 'dp', 0, 0)  17.3 us
    all_to_all x2, waiting for transfers between devices, on_device(): arrived.append(lax.all_to_all(moved, 'dp', 0, 0).reshape(rows, step))  13.9 us
    dot_general x2, matrix products, on_device(): jnp.dot(mixed, w_out[:, span], preferred_element_type=jnp.float32)  13.3 us
    dot_general x1, matrix products, on_device(): jnp.dot(piece, w_query, preferred_element_type=jnp.float32) + q_shift  13 us
    all_to_all x2, starting transfers between devices, on_device(): arrived.append(lax.all_to_all(moved, 'dp', 0, 0).reshape(rows, step))  9.34 us
    unnamed x42, local copies, waits for them, and re-layouts  9.06 us
  transfers between devices with their start and end apart: 8, of which 6 were waited for; matrix products, arithmetic and copies ran while one was open for 7% of the time, Pallas kernels for 0%

profile of v1, /device:TPU:2, one launch (start us, length us, event | category | flops | bytes accessed | tf_op | source)
XLA Modules:
  0.0 248.4 jit_solution(12601674396309996593)
XLA Ops:
  1.5 2.3 multiply_reduce_fusion
  3.9 2.3 multiply_convert_fusion
  8.8 7.9 %copy.39 = bf16[512,5120]{1,0:T(8,128)(2,1)} copy(bf16[512,5120]{0,1:T(8,128)(2,1)} %bitcast.77) | data formatting | bytes 10485760 | tf_op jit(solution)/shard_map/dot_general | solution.py:84
  17.6 3.3 %broadcast_select_fusion.1 = (bf16[256,5120]{1,0:T(8,128)(2,1)S(1)}, bf16[256,5120]{1,0:T(8,128)(2,1)S(1)}) fusion(bf16[256,5120]{1,0:T(8,128)(2,1)} %collective-permute-done, pred[]{:T(512)S(6)} %eq.46, f32[5120]{0:T(1024)S(1)} %bitcast.82, f32[256]{0:T(256)S(1)} %add_rsqrt_fusion, bf16[1,1,256,1,5120]{4,2,3,1,0:T(8,128)(2,1)S(1)} %copy-done), kind=kLoop, calls=%fused_computation.38 | loop fusion | flops 7864320 | bytes 10507265 | tf_op jit(solution)/shard_map/jit(_where)/select_n | solution.py:80
  23.3 13.0 %fusion.22 = f32[512,1536]{1,0:T(8,128)} fusion(bf16[1,5120,1536]{2,1,0:T(8,128)(2,1)} %param.17, f32[1536]{0:T(1024)S(1)} %convert_reduce_fusion.1, bf16[256,5120]{1,0:T(8,128)(2,1)S(1)} %get-tuple-element.20, bf16[256,5120]{1,0:T(8,128)(2,1)S(1)} %get-tuple-element.19), kind=kOutput, calls=%fused_computation.26 | convolution fusion | flops 8064335872 | bytes 24123392 | tf_op jit(solution)/shard_map/dot_general | solution.py:83
  36.3 3.5 %copy.29 = f32[512,1536]{0,1:T(8,128)} copy(f32[512,1536]{1,0:T(8,128)} %fusion.22) | data formatting | bytes 6291456 | tf_op jit(solution)/shard_map/add | solution.py:83
  39.9 4.0 %fusion.47 = (f32[512,4,3,64]{0,3,2,1:T(8,128)}, f32[512,4,3,64]{0,3,2,1:T(8,128)}) fusion(f32[512,4,3,128]{0,3,2,1:T(8,128)} %bitcast.76), kind=kLoop, calls=%fused_computation.87 | loop fusion | bytes 6291456 | tf_op jit(solution)/shard_map/slice | solution.py:29
  43.9 3.3 %copy.43 = f32[512,4,3,64]{3,0,2,1:T(8,128)} copy(f32[512,4,3,64]{0,3,2,1:T(8,128)} %get-tuple-element.21) | data formatting | bytes 3145728
  47.2 3.4 %copy.42 = f32[512,4,3,64]{3,0,2,1:T(8,128)} copy(f32[512,4,3,64]{0,3,2,1:T(8,128)} %get-tuple-element.22) | data formatting | bytes 3145728
  50.6 7.1 %fusion.12 = f32[512,4,128]{0,2,1:T(8,128)S(1)} fusion(bf16[4,128,5120]{2,1,0:T(8,128)(2,1)} %bitcast.78, bf16[256,5120]{1,0:T(8,128)(2,1)} %copy-done.5, bf16[256,5120]{1,0:T(8,128)(2,1)} %copy-done.3), kind=kOutput, calls=%fused_computation.18 | convolution fusion | flops 2694840320 | bytes 11534336 | tf_op jit(solution)/shard_map/dot_general | solution.py:84
  57.9 6.4 %fusion.33 = bf16[512,512]{0,1:T(8,128)(2,1)} fusion(bf16[1,5120,512]{2,1,0:T(8,128)(2,1)} %param.20, bf16[256,5120]{1,0:T(8,128)(2,1)S(1)} %copy-done.6, bf16[256,5120]{1,0:T(8,128)(2,1)S(1)} %copy-done.4, f32[512]{0:T(512)S(1)} %bitcast.83), kind=kOutput, calls=%fused_computation.47 | convolution fusion | flops 2695364608 | bytes 11012096 | tf_op jit(solution)/shard_map/dot_general | solution.py:85
  67.2 8.2 %fusion.48 = (f32[4,3,512]{2,1,0:T(4,128)S(1)}, f32[4,3,512,512]{2,3,1,0:T(8,128)}) fusion(f32[4,512,512,3]{2,1,3,0:T(8,128)S(1)} %fusion.26, pred[512,512]{0,1:T(8,128)(4,1)S(1)} %copy-done.9), kind=kOutput, calls=%fused_computation.88 | output fusion | flops 18874880 | bytes 25452544 | tf_op jit(solution)/shard_map/sub | solution.py:101
  75.5 5.7 %fusion.25 = bf16[4,128,3,512]{3,1,2,0:T(8,128)(2,1)S(1)} fusion(bf16[512,4,128,1]{0,2,3,1:T(8,128)(2,1)S(1)} %bitcast.93, f32[4,3,512,512]{2,3,1,0:T(8,128)} %get-tuple-element.32, f32[4,3,512]{2,1,0:T(4,128)S(1)} %get-tuple-element.31), kind=kOutput, calls=%fused_computation.39 | convolution fusion | flops 812384256 | bytes 14704640 | tf_op jit(solution)/shard_map/gpqk,kgh->qgph/dot_general | solution.py:103
  81.2 8.5 %fusion.19 = bf16[512,2560]{1,0:T(8,128)(2,1)S(1)} fusion(bf16[512,1536]{0,1:T(8,128)(2,1)S(1)} %bitcast.91, bf16[1536,5120]{1,0:T(8,128)(2,1)} %bitcast.87), kind=kOutput, calls=%fused_computation.25 | convolution fusion | flops 4027842560 | bytes 12058624 | tf_op jit(solution)/shard_map/dot_general | solution.py:118
  89.8 4.7 %fusion.16 = bf16[512,2560]{1,0:T(8,128)(2,1)S(1)} fusion(bf16[512,1536]{0,1:T(8,128)(2,1)S(1)} %bitcast.92, bf16[1536,5120]{1,0:T(8,128)(2,1)S(1)} %bitcast.90), kind=kOutput, calls=%fused_computation.24 | convolution fusion | flops 4027842560 | bytes 12058624 | tf_op jit(solution)/shard_map/dot_general | solution.py:118
  99.8 3.0 %fusion.46 = (bf16[256,2560]{1,0:T(8,128)(2,1)}, f32[256,2560]{1,0:T(8,128)S(1)}, bf16[256,2560]{1,0:T(8,128)(2,1)S(1)}, f32[256,2560]{1,0:T(8,128)}) fusion(bf16[256,2560]{1,0:T(8,128)(2,1)S(1)} %collective-permute-done.2, bf16[512,2560]{1,0:T(8,128)(2,1)S(1)} %fusion.19, s32[]{:T(128)S(6)} %select_n.50, f32[256,5120]{1,0:T(8,128)S(1)} %bitcast_convert_fusion, ...), kind=kLoop, calls=%fused_computation.86 | loop fusion | flops 6553600 | bytes 18350084 | tf_op jit(solution)/shard_map/convert_element_type | solution.py:127
  102.8 28.6 %all_to_all.20 = bf16[16,16,2560]{2,1,0:T(8,128)(2,1)} all-to-all(bf16[16,16,2560]{2,1,0:T(8,128)(2,1)S(1)} %bitcast.80), channel_id=1, replica_groups=mesh['section'=4,'dp'=16,'tensor'=2] {'dp'}, dimensions={0} | all-to-all | bytes 2621440 | tf_op jit(solution)/shard_map/all_to_all | solution.py:128
  131.4 4.4 %all-to-all-start.2 = ((bf16[16,16,2560]{2,1,0:T(8,128)(2,1)}), bf16[16,16,2560]{2,1,0:T(8,128)(2,1)}, u32[]{:S(2)}, u32[]{:S(2)}) async-start(bf16[16,16,2560]{2,1,0:T(8,128)(2,1)} %bitcast.79), calls=%async_computation.2 | async-start | bytes 2621440 | tf_op jit(solution)/shard_map/all_to_all | solution.py:128
  135.9 3.0 %gather_fusion = bf16[16,16,2560]{2,1,0:T(8,128)(2,1)} fusion(bf16[16,16,2560]{2,1,0:T(8,128)(2,1)} %all_to_all.20, s32[1024]{0:T(1024)S(1)} %pad_clamp_fusion), kind=kCustom, calls=%fused_computation.clone | custom fusion | bytes 2621504 | tf_op jit(solution)/shard_map/jit(_take)/gather | solution.py:129
  138.9 17.3 %all-to-all-done.2 = bf16[16,16,2560]{2,1,0:T(8,128)(2,1)} async-done(((bf16[16,16,2560]{2,1,0:T(8,128)(2,1)}), bf16[16,16,2560]{2,1,0:T(8,128)(2,1)}, u32[]{:S(2)}, u32[]{:S(2)}) %all-to-all-start.2) | async-done | bytes 1310752 | tf_op jit(solution)/shard_map/all_to_all | solution.py:128
  156.2 3.0 %gather_fusion.1 = bf16[16,16,2560]{2,1,0:T(8,128)(2,1)} fusion(bf16[16,16,2560]{2,1,0:T(8,128)(2,1)} %all-to-all-done.2, s32[1024]{0:T(1024)S(1)} %pad_clamp_fusion), kind=kCustom, calls=%fused_computation.1.clone | custom fusion | bytes 2621504 | tf_op jit(solution)/shard_map/jit(_take)/gather | solution.py:129
  159.2 3.1 %select_select_fusion.1 = (bf16[16,16,2560]{2,1,0:T(8,128)(2,1)}, bf16[16,16,2560]{2,1,0:T(8,128)(2,1)S(1)}) fusion(bf16[16,16,2560]{2,1,0:T(8,128)(2,1)} %gather_fusion, pred[16]{0:T(512)(128)(4,1)S(1)} %get-tuple-element.11, pred[16]{0:T(512)(128)(4,1)S(1)} %compare_bitcast_fusion, bf16[16,16,2560]{2,1,0:T(8,128)(2,1)} %gather_fusion.1), kind=kLoop, calls=%fused_computation.46 | loop fusion | flops 2621440 | bytes 5242912 | tf_op jit(solution)/shard_map/jit(_where)/select_n | solution.py:130
  162.3 3.4 %collective-permute-start.4 = (bf16[16,16,2560]{2,1,0:T(8,128)(2,1)S(1)}, bf16[16,16,2560]{2,1,0:T(8,128)(2,1)}, u32[]{:S(2)}, u32[]{:S(2)}) collective-permute-start(bf16[16,16,2560]{2,1,0:T(8,128)(2,1)S(1)} %get-tuple-element.28), channel_id=1, source_target_pairs={{0,32},{32,64},{64,96},{1,33},{33,65},{65,97},{2,34},{34,66},{66,9... | collective-permute-start | bytes 3932168 | tf_op jit(solution)/shard_map/ppermute | solution.py:131
  165.7 3.1 %collective-permute-start.3 = (bf16[16,16,2560]{2,1,0:T(8,128)(2,1)}, bf16[16,16,2560]{2,1,0:T(8,128)(2,1)}, u32[]{:S(2)}, u32[]{:S(2)}) collective-permute-start(bf16[16,16,2560]{2,1,0:T(8,128)(2,1)} %get-tuple-element.27), channel_id=1, source_target_pairs={{0,32},{32,64},{64,96},{1,33},{33,65},{65,97},{2,34},{34,66},{66,9... | collective-permute-start | bytes 3932168 | tf_op jit(solution)/shard_map/ppermute | solution.py:131
  168.9 27.2 %collective-permute-done.4 = bf16[16,16,2560]{2,1,0:T(8,128)(2,1)} collective-permute-done((bf16[16,16,2560]{2,1,0:T(8,128)(2,1)S(1)}, bf16[16,16,2560]{2,1,0:T(8,128)(2,1)}, u32[]{:S(2)}, u32[]{:S(2)}) %collective-permute-start.4) | collective-permute-done | bytes 1310752 | tf_op jit(solution)/shard_map/ppermute | solution.py:131
  196.0 4.4 %all-to-all-start.3 = ((bf16[16,16,2560]{2,1,0:T(8,128)(2,1)}), bf16[16,16,2560]{2,1,0:T(8,128)(2,1)}, u32[]{:S(2)}, u32[]{:S(2)}) async-start(bf16[16,16,2560]{2,1,0:T(8,128)(2,1)} %collective-permute-done.4), calls=%async_computation.3 | async-start | bytes 2621440 | tf_op jit(solution)/shard_map/all_to_all | solution.py:132
  200.4 19.8 %collective-permute-done.3 = bf16[16,16,2560]{2,1,0:T(8,128)(2,1)} collective-permute-done((bf16[16,16,2560]{2,1,0:T(8,128)(2,1)}, bf16[16,16,2560]{2,1,0:T(8,128)(2,1)}, u32[]{:S(2)}, u32[]{:S(2)}) %collective-permute-start.3) | collective-permute-done | bytes 1310752 | tf_op jit(solution)/shard_map/ppermute | solution.py:131
  220.2 5.0 %all-to-all-start.1 = ((bf16[16,16,2560]{2,1,0:T(8,128)(2,1)}), bf16[16,16,2560]{2,1,0:T(8,128)(2,1)}, u32[]{:S(2)}, u32[]{:S(2)}) async-start(bf16[16,16,2560]{2,1,0:T(8,128)(2,1)} %collective-permute-done.3), calls=%async_computation.1 | async-start | bytes 2621440 | tf_op jit(solution)/shard_map/all_to_all | solution.py:132
  225.3 2.6 %multiply_reduce_fusion.3 = (f32[256]{0:T(256)S(1)}, f32[256]{0:T(256)S(1)}, f32[256]{0:T(256)S(1)}, f32[256]{0:T(256)S(1)}) fusion(f32[256,2560]{1,0:T(8,128)S(1)} %get-tuple-element.14, f32[2560]{0:T(1024)S(1)} %get-tuple-element.7, f32[256,2560]{1,0:T(8,128)} %get-tuple-element.18, f32[2560]{0:T(1024)S(1)} %get-tuple-element.8), kind=kLoop, calls=%fused_computation.35 | loop fusion | flops 5241856 | bytes 5267456 | tf_op jit(solution)/shard_map/reduce_sum | solution.py:126
  228.1 3.0 %psum.7 = f32[1,1,1,4]{3,2,1,0:T(1,128)} all-reduce(f32[1,1,1,4]{3,2,1,0:T(1,128)S(1)} %bitcast.86), channel_id=1, replica_groups=mesh['section'=4,'dp'=16,'tensor'=2] {'tensor'}, use_global_device_ids=true, to_apply=%region_11.12 | all-reduce | flops 4 | bytes 32 | tf_op jit(solution)/shard_map/psum | solution.py:137
  231.1 13.9 %all-to-all-done.1 = bf16[16,16,2560]{2,1,0:T(8,128)(2,1)} async-done(((bf16[16,16,2560]{2,1,0:T(8,128)(2,1)}), bf16[16,16,2560]{2,1,0:T(8,128)(2,1)}, u32[]{:S(2)}, u32[]{:S(2)}) %all-to-all-start.1) | async-done | bytes 1310752 | tf_op jit(solution)/shard_map/all_to_all | solution.py:132
  244.9 3.5 %maximum_bitcast_fusion = bf16[1,1,256,1,5120]{4,2,3,1,0:T(8,128)(2,1)} fusion(bf16[256,2560]{1,0:T(8,128)(2,1)} %bitcast.29, bf16[256,2560]{1,0:T(8,128)(2,1)} %bitcast.27), kind=kLoop, calls=%fused_computation.31 | loop fusion | flops 5242880 | bytes 5242880 | tf_op jit(solution)/shard_map/broadcast_in_dim | solution.py:139
  (76 shorter events, 15.4 us)
Async XLA Ops:
  0.6 3.3 %copy-start = (bf16[1,1,256,1,5120]{4,2,3,1,0:T(8,128)(2,1)S(1)}, bf16[1,1,256,1,5120]{4,2,3,1,0:T(8,128)(2,1)}, u32[]{:S(2)}) copy-start(bf16[1,1,256,1,5120]{4,2,3,1,0:T(8,128)(2,1)} %param.13) | copy-start | bytes 7864324
  3.9 2.3 copy-start.12
  3.9 2.3 copy-start.13
  6.2 11.4 %collective-permute-start = (bf16[256,5120]{1,0:T(8,128)(2,1)}, bf16[256,5120]{1,0:T(8,128)(2,1)}, u32[]{:S(2)}, u32[]{:S(2)}) collective-permute-start(bf16[256,5120]{1,0:T(8,128)(2,1)} %multiply_convert_fusion), channel_id=1, source_target_pairs={{0,1},{1,0},{2,3},{3,2},{4,5},{5,4},{6,7},{7,6},{8,9},{9,8},{10,11... | collective-permute-start | bytes 7864328 | tf_op jit(solution)/shard_map/ppermute | solution.py:46
  8.8 7.9 %copy-start.11 = (bf16[1,1536]{1,0:T(2,128)(2,1)S(1)}, bf16[1,1536]{1,0:T(2,128)(2,1)}, u32[]{:S(2)}) copy-start(bf16[1,1536]{1,0:T(2,128)(2,1)} %param.18) | copy-start | bytes 9220
  20.9 1.6 copy-start.3
  20.9 2.3 copy-start.5
  50.6 7.3 %copy-start.4 = (bf16[256,5120]{1,0:T(8,128)(2,1)S(1)}, bf16[256,5120]{1,0:T(8,128)(2,1)}, u32[]{:S(2)}) copy-start(bf16[256,5120]{1,0:T(8,128)(2,1)} %copy-done.3) | copy-start | bytes 7864324
  50.6 7.3 %copy-start.6 = (bf16[256,5120]{1,0:T(8,128)(2,1)S(1)}, bf16[256,5120]{1,0:T(8,128)(2,1)}, u32[]{:S(2)}) copy-start(bf16[256,5120]{1,0:T(8,128)(2,1)} %copy-done.5) | copy-start | bytes 7864324
  57.9 6.4 %copy-start.1 = (f32[512,4,3,64]{3,0,2,1:T(8,128)S(1)}, f32[512,4,3,64]{3,0,2,1:T(8,128)}, u32[]{:S(2)}) copy-start(f32[512,4,3,64]{3,0,2,1:T(8,128)} %copy.43) | copy-start | bytes 4718596
  57.9 6.4 %copy-start.2 = (f32[512,4,3,64]{3,0,2,1:T(8,128)S(1)}, f32[512,4,3,64]{3,0,2,1:T(8,128)}, u32[]{:S(2)}) copy-start(f32[512,4,3,64]{3,0,2,1:T(8,128)} %copy.42) | copy-start | bytes 4718596
  57.9 6.4 %copy-start.7 = (f32[512,64]{1,0:T(8,128)S(1)}, f32[512,64]{1,0:T(8,128)}, u32[]{:S(2)}) copy-start(f32[512,64]{1,0:T(8,128)} %copy.33) | copy-start | bytes 393220
  57.9 6.4 %copy-start.8 = (f32[512,64]{1,0:T(8,128)S(1)}, f32[512,64]{1,0:T(8,128)}, u32[]{:S(2)}) copy-start(f32[512,64]{1,0:T(8,128)} %copy.31) | copy-start | bytes 393220
  65.1 2.0 copy-start.9
  67.2 8.2 %copy-start.15 = (bf16[512,512]{0,1:T(8,128)(2,1)S(1)}, bf16[512,512]{0,1:T(8,128)(2,1)}, u32[]{:S(2)}) copy-start(bf16[512,512]{0,1:T(8,128)(2,1)} %fusion.33) | copy-start | bytes 1572868
  75.4 14.3 %slice-start = ((s8[15728640]{0:T(1024)(128)(4,1)}), s8[4194304]{0:T(1024)(128)(4,1)S(1)}, s32[]{:S(2)}) async-start(s8[15728640]{0:T(1024)(128)(4,1)} %bitcast.88), calls=%async_computation.4 | async-start | bytes 8388608
  75.4 14.3 %slice-start.1 = ((s8[15728640]{0:T(1024)(128)(4,1)}), s8[4194304]{0:T(1024)(128)(4,1)S(1)}, s32[]{:S(2)}) async-start(s8[15728640]{0:T(1024)(128)(4,1)} %bitcast.88), calls=%async_computation.5 | async-start | bytes 8388608
  75.4 14.3 %slice-start.2 = ((s8[15728640]{0:T(1024)(128)(4,1)}), s8[4194304]{0:T(1024)(128)(4,1)S(1)}, s32[]{:S(2)}) async-start(s8[15728640]{0:T(1024)(128)(4,1)} %bitcast.88), calls=%async_computation.6 | async-start | bytes 8388608
  81.2 8.6 %slice-start.3 = ((s8[15728640]{0:T(1024)(128)(4,1)}), s8[3145728]{0:T(1024)(128)(4,1)S(1)}, s32[]{:S(2)}) async-start(s8[15728640]{0:T(1024)(128)(4,1)} %bitcast.88), calls=%async_computation.7 | async-start | bytes 6291456
  94.6 3.2 %collective-permute-start.2 = (bf16[256,2560]{1,0:T(8,128)(2,1)S(1)}, bf16[256,2560]{1,0:T(8,128)(2,1)S(1)}, u32[]{:S(2)}, u32[]{:S(2)}) collective-permute-start(bf16[256,2560]{1,0:T(8,128)(2,1)S(1)} %constant_dynamic-slice_fusion.1), channel_id=1, source_target_pairs={{0,1},{1,0},{2,3},{3,2},{4,5},{5,4},{6,7},{7,6},{8,9},{9,8},{10,11... | collective-permute-start | bytes 3932168 | tf_op jit(solution)/shard_map/ppermute | solution.py:46
  95.3 4.4 %collective-permute-start.1 = (bf16[256,2560]{1,0:T(8,128)(2,1)S(1)}, bf16[256,2560]{1,0:T(8,128)(2,1)S(1)}, u32[]{:S(2)}, u32[]{:S(2)}) collective-permute-start(bf16[256,2560]{1,0:T(8,128)(2,1)S(1)} %constant_dynamic-slice_fusion.2), channel_id=1, source_target_pairs={{0,1},{1,0},{2,3},{3,2},{4,5},{5,4},{6,7},{7,6},{8,9},{9,8},{10,11... | collective-permute-start | bytes 3932168 | tf_op jit(solution)/shard_map/ppermute | solution.py:46
  102.8 33.0 %copy-start.14 = (s32[3,16]{1,0:T(4,128)S(1)}, s32[3,16]{1,0:T(4,128)}, u32[]{:S(2)}) copy-start(s32[3,16]{1,0:T(4,128)} %param.15) | copy-start | bytes 580
  131.4 24.7 %all-to-all-start.2 = ((bf16[16,16,2560]{2,1,0:T(8,128)(2,1)}), bf16[16,16,2560]{2,1,0:T(8,128)(2,1)}, u32[]{:S(2)}, u32[]{:S(2)}) async-start(bf16[16,16,2560]{2,1,0:T(8,128)(2,1)} %bitcast.79), calls=%async_computation.2 | async-start | bytes 2621440 | tf_op jit(solution)/shard_map/all_to_all | solution.py:128
  162.3 33.7 %collective-permute-start.4 = (bf16[16,16,2560]{2,1,0:T(8,128)(2,1)S(1)}, bf16[16,16,2560]{2,1,0:T(8,128)(2,1)}, u32[]{:S(2)}, u32[]{:S(2)}) collective-permute-start(bf16[16,16,2560]{2,1,0:T(8,128)(2,1)S(1)} %get-tuple-element.28), channel_id=1, source_target_pairs={{0,32},{32,64},{64,96},{1,33},{33,65},{65,97},{2,34},{34,66},{66,9... | collective-permute-start | bytes 3932168 | tf_op jit(solution)/shard_map/ppermute | solution.py:131
  165.7 59.5 %copy-start.10 = (bf16[1,5120]{1,0:T(2,128)(2,1)S(1)}, bf16[1,5120]{1,0:T(2,128)(2,1)}, u32[]{:S(2)}) copy-start(bf16[1,5120]{1,0:T(2,128)(2,1)} %param.23) | copy-start | bytes 30724
  165.7 54.5 %collective-permute-start.3 = (bf16[16,16,2560]{2,1,0:T(8,128)(2,1)}, bf16[16,16,2560]{2,1,0:T(8,128)(2,1)}, u32[]{:S(2)}, u32[]{:S(2)}) collective-permute-start(bf16[16,16,2560]{2,1,0:T(8,128)(2,1)} %get-tuple-element.27), channel_id=1, source_target_pairs={{0,32},{32,64},{64,96},{1,33},{33,65},{65,97},{2,34},{34,66},{66,9... | collective-permute-start | bytes 3932168 | tf_op jit(solution)/shard_map/ppermute | solution.py:131
  196.0 24.2 %all-to-all-start.3 = ((bf16[16,16,2560]{2,1,0:T(8,128)(2,1)}), bf16[16,16,2560]{2,1,0:T(8,128)(2,1)}, u32[]{:S(2)}, u32[]{:S(2)}) async-start(bf16[16,16,2560]{2,1,0:T(8,128)(2,1)} %collective-permute-done.4), calls=%async_computation.3 | async-start | bytes 2621440 | tf_op jit(solution)/shard_map/all_to_all | solution.py:132
  220.2 24.7 %all-to-all-start.1 = ((bf16[16,16,2560]{2,1,0:T(8,128)(2,1)}), bf16[16,16,2560]{2,1,0:T(8,128)(2,1)}, u32[]{:S(2)}, u32[]{:S(2)}) async-start(bf16[16,16,2560]{2,1,0:T(8,128)(2,1)} %collective-permute-done.3), calls=%async_computation.1 | async-start | bytes 2621440 | tf_op jit(solution)/shard_map/all_to_all | solution.py:132

commit v2 on v1

v2 whole, which is shorter than its diff:
```python
import functools
import jax
import jax.numpy as jnp
from jax import lax
from jax.experimental import pallas as pl
from jax.experimental.pallas import tpu as pltpu
from jax.sharding import PartitionSpec as P

HD = 128
TILE = 512
AHEAD = 8
CHUNKS = (3072, 2048)
VMEM = 60 * 1024 * 1024

epsilon = 1e-06
rope_base = 1000000.0


def ends_of(lengths):
    ends = []
    total = 0
    for i in range(lengths.shape[0]):
        total = total + lengths[i]
        ends.append(total)
    return ends


def starts_at(places, ends):
    start = jnp.zeros_like(places)
    for end in ends[:-1]:
        start = jnp.where(places >= end, end, start)
    return start


def swap(value):
    return lax.ppermute(value, "tensor", [(0, 1), (1, 0)])


def qkv_kernel(half, lengths, gain_ref, q_bias_ref, v_bias_ref, x, wq, wk, wv, *rest):
    out, held, normed, weights, ready, turns, x_sems, w_sems, out_sems = rest[-9:]
    rows, width = x.shape
    slots, deep = weights.shape[:2]
    tiles = []
    for source in (wq, wk, wv):
        for at in range(0, source.shape[1], TILE):
            tiles.append((source, at))
    n_query = wq.shape[1] // TILE
    n_rope = n_query + wk.shape[1] // TILE
    few = rows // 4
    parts = width // deep
    total = len(tiles) * parts

    def x_copy(r):
        here = pl.ds(r * few, few)
        return pltpu.make_async_copy(x.at[here], held.at[here], x_sems.at[r])

    def w_copy(j):
        source, at = tiles[j // parts]
        d = j % parts
        return pltpu.make_async_copy(
            source.at[d * deep : (d + 1) * deep, at : at + TILE],
            weights.at[j % slots],
            w_sems.at[j % slots],
        )

    def out_copy(t):
        return pltpu.make_async_copy(
            ready.at[:, t * TILE : (t + 1) * TILE],
            out.at[
                pl.ds(pl.multiple_of(half[0] * rows, rows), rows), t * TILE : (t + 1) * TILE
            ],
            out_sems.at[t],
        )

    for r in range(4):
        x_copy(r).start()
    for j in range(parts):
        w_copy(j).start()
    places = half[0] * rows + lax.broadcasted_iota(jnp.int32, (rows, HD), 0)
    offset = (places - starts_at(places, ends_of(lengths))).astype(jnp.float32)
    lane = lax.broadcasted_iota(jnp.int32, (1, HD), 1)
    order = (lane % (HD // 2)).astype(jnp.float32) * 2.0
    angle = offset * jnp.exp(-jnp.log(rope_base) * order / HD)
    turns[0] = jnp.cos(angle)
    turns[1] = jnp.where(lane < HD // 2, -1.0, 1.0) * jnp.sin(angle)
    for r in range(4):
        x_copy(r).wait()
        if r == 0:
            for j in range(parts, AHEAD):
                w_copy(j).start()
        for at in range(r * few, (r + 1) * few, 16):
            v = held[at : at + 16, :].astype(jnp.float32)
            factor = lax.rsqrt(jnp.mean(v * v, axis=-1, keepdims=True) + epsilon)
            normed[at : at + 16, :] = (
                v * factor * gain_ref[...].astype(jnp.float32)
            ).astype(jnp.bfloat16)

    for t in range(len(tiles)):
        for d in range(parts):
            w_copy(t * parts + d).wait()
        for j in range(t * parts + AHEAD, min((t + 1) * parts + AHEAD, total)):
            w_copy(j).start()
        part = None
        for d in range(parts):
            term = jnp.dot(
                normed[:, d * deep : (d + 1) * deep],
                weights[(t * parts + d) % slots],
                preferred_element_type=jnp.float32,
            )
            part = term if part is None else part + term
        here = slice(t * TILE, (t + 1) * TILE)
        if t < n_query:
            part = part + q_bias_ref[:, here].astype(jnp.float32)
        elif t >= n_rope:
            there = slice((t - n_rope) * TILE, (t - n_rope + 1) * TILE)
            part = part + v_bias_ref[:, there].astype(jnp.float32)
        if t < n_rope:
            for at in range(0, TILE, HD):
                u = part[:, at : at + HD]
                turned = u * turns[0] + pltpu.roll(u, HD // 2, 1) * turns[1]
                ready[:, t * TILE + at : t * TILE + at + HD] = turned.astype(jnp.bfloat16)
        else:
            ready[:, here] = part.astype(jnp.bfloat16)
        out_copy(t).start()
    for t in range(len(tiles)):
        out_copy(t).wait()


def qkv_half(half, lengths, x, gain, q_bias, v_bias, wq, wk, wv, held):
    rows, width = x.shape
    columns = wq.shape[1] + wk.shape[1] + wv.shape[1]
    n = columns // TILE
    whole = pl.BlockSpec(memory_space=pltpu.HBM)
    operands = [gain, q_bias, v_bias, x, wq, wk, wv]
    specs = [pl.BlockSpec(v.shape, lambda i, h, l: (0, 0)) for v in operands[:3]] + [whole] * 4
    aliases = {}
    if held is not None:
        operands.append(held)
        specs.append(whole)
        aliases = {len(operands) + 1: 0}
    return pl.pallas_call(
        qkv_kernel,
        grid_spec=pltpu.PrefetchScalarGridSpec(
            num_scalar_prefetch=2,
            grid=(1,),
            in_specs=specs,
            out_specs=whole,
            scratch_shapes=[
                pltpu.VMEM((rows, width), jnp.bfloat16),
                pltpu.VMEM((rows, width), jnp.bfloat16),
                pltpu.VMEM((AHEAD + 5, width // 5, TILE), jnp.bfloat16),
                pltpu.VMEM((rows, columns), jnp.bfloat16),
                pltpu.VMEM((2, rows, HD), jnp.float32),
                pltpu.SemaphoreType.DMA((4,)),
                pltpu.SemaphoreType.DMA((AHEAD + 5,)),
                pltpu.SemaphoreType.DMA((n,)),
            ],
        ),
        out_shape=jax.ShapeDtypeStruct((2 * rows, columns), jnp.bfloat16),
        input_output_aliases=aliases,
        compiler_params=pltpu.CompilerParams(vmem_limit_bytes=VMEM),
        cost_estimate=pl.CostEstimate(
            flops=2 * rows * width * columns,
            bytes_accessed=2 * width * columns,
            transcendentals=0,
        ),
        name="qkv",
    )(half, lengths, *operands)


def attention_kernel(lengths, q_ref, k_ref, v_ref, out_ref):
    ends = ends_of(lengths)
    length = k_ref.shape[0]
    groups = k_ref.shape[1] // HD
    heads = q_ref.shape[1] // HD // groups
    block = 128
    for i in range(length // block):
        lo = max(0, i - 2) * block
        hi = (i + 1) * block
        here = slice(i * block, hi)
        b = lo + lax.broadcasted_iota(jnp.int32, (hi - lo, block), 0)
        a = i * block + lax.broadcasted_iota(jnp.int32, (hi - lo, block), 1)
        start = starts_at(i * block + lax.broadcasted_iota(jnp.int32, (1, block), 1), ends)
        allowed = (b <= a) & (b >= start)
        allowed = jnp.concatenate([allowed] * heads, axis=1)
        for g in range(groups):
            at = g * HD
            q = jnp.concatenate([q_ref[here, (g * heads + h) * HD : (g * heads + h + 1) * HD] for h in range(heads)], axis=0)
            logits = lax.dot_general(
                k_ref[lo:hi, at:at+HD], q, (((1,), (1,)), ((), ())), preferred_element_type=jnp.float32
            ) * HD ** (-0.5)
            logits = jnp.where(allowed, logits, -1e30)
            expons = jnp.exp(logits - jnp.max(logits, axis=0, keepdims=True))
            probs = expons * (1.0 / jnp.sum(expons, axis=0, keepdims=True))
            mixed = lax.dot_general(
                probs.astype(jnp.bfloat16), v_ref[lo:hi, at:at+HD], (((0,), (0,)), ((), ())), preferred_element_type=jnp.float32
            ).astype(jnp.bfloat16)
            for h in range(heads):
                out_ref[here, (g * heads + h) * HD : (g * heads + h + 1) * HD] = mixed[h * block : (h + 1) * block]


def attention(lengths, qkv, q_width, k_width):
    length = qkv.shape[0]
    pace = 2
    groups = k_width // HD
    steps = groups // pace
    wide = q_width // steps
    deep = k_width // steps
    return pl.pallas_call(
        attention_kernel,
        grid_spec=pltpu.PrefetchScalarGridSpec(
            num_scalar_prefetch=1,
            grid=(steps,),
            in_specs=[
                pl.BlockSpec((length, wide), lambda g, l: (0, g)),
                pl.BlockSpec((length, deep), lambda g, l: (0, q_width // deep + g)),
                pl.BlockSpec((length, deep), lambda g, l: (0, (q_width + k_width) // deep + g)),
            ],
            out_specs=pl.BlockSpec((length, wide), lambda g, l: (0, g)),
        ),
        out_shape=jax.ShapeDtypeStruct((length, q_width), jnp.bfloat16),
        compiler_params=pltpu.CompilerParams(vmem_limit_bytes=VMEM),
        cost_estimate=pl.CostEstimate(
            flops=8 * length * length * q_width,
            bytes_accessed=8 * length * q_width,
            transcendentals=length * length,
        ),
        name="attention",
    )(lengths, qkv, qkv, qkv)


def out_kernel(at, half, mixed, w, mine, theirs, held, weights, term, m_sems, w_sems, out_sems):
    length, depth = mixed.shape
    rows, wide = mine.shape
    few, deep = length // 4, depth // 3

    def m_copy(r):
        here = slice(r * few, (r + 1) * few)
        return pltpu.make_async_copy(mixed.at[here], held.at[here], m_sems.at[r])

    def w_copies(t):
        return [
            pltpu.make_async_copy(
                w.at[d * deep : (d + 1) * deep, at + t * TILE : at + (t + 1) * TILE],
                weights.at[t, d * deep : (d + 1) * deep],
                w_sems.at[t, d],
            )
            for d in range(3)
        ]

    def out_copies(t):
        here = slice(t * TILE, (t + 1) * TILE)
        return [
            pltpu.make_async_copy(
                term.at[pl.ds(pl.multiple_of(place * rows, rows), rows), here],
                target.at[:, here],
                out_sems.at[t, i],
            )
            for i, (place, target) in enumerate(((1 - half[0], theirs), (half[0], mine)))
        ]

    n = wide // TILE
    for r in range(4):
        m_copy(r).start()
    for t in range(n):
        for copy in w_copies(t):
            copy.start()
    for r in range(4):
        m_copy(r).wait()
    for t in range(n):
        for copy in w_copies(t):
            copy.wait()
        term[:, t * TILE : (t + 1) * TILE] = jnp.dot(
            held[...], weights[t], preferred_element_type=jnp.float32
        ).astype(jnp.bfloat16)
        for copy in out_copies(t):
            copy.start()
    for t in range(n):
        for copy in out_copies(t):
            copy.wait()


def out_project(half, mixed, w_out, at, wide):
    length, depth = mixed.shape
    n = wide // TILE
    result = jax.ShapeDtypeStruct((length // 2, wide), jnp.bfloat16)
    whole = pl.BlockSpec(memory_space=pltpu.HBM)
    return pl.pallas_call(
        functools.partial(out_kernel, at),
        grid_spec=pltpu.PrefetchScalarGridSpec(
            num_scalar_prefetch=1,
            grid=(1,),
            in_specs=[whole, whole],
            out_specs=[whole, whole],
            scratch_shapes=[
                pltpu.VMEM((length, depth), jnp.bfloat16),
                pltpu.VMEM((n, depth, TILE), jnp.bfloat16),
                pltpu.VMEM((length, wide), jnp.bfloat16),
                pltpu.SemaphoreType.DMA((4,)),
                pltpu.SemaphoreType.DMA((n, 3)),
                pltpu.SemaphoreType.DMA((n, 2)),
            ],
        ),
        out_shape=[result, result],
        compiler_params=pltpu.CompilerParams(vmem_limit_bytes=VMEM),
        cost_estimate=pl.CostEstimate(
            flops=2 * length * depth * wide,
            bytes_accessed=2 * depth * wide,
            transcendentals=0,
        ),
        name="out_project",
    )(half, mixed, w_out)


def score_kernel(half, lengths, rating_ref, x, *rest):
    n = len(CHUNKS)
    mines, theirs, (out_ref, held, terms, sems) = rest[:n], rest[n : 2 * n], rest[2 * n :]
    rows, width = x.shape
    last = [end - 1 - half[0] * rows for end in ends_of(lengths)]

    def copies(i):
        row = jnp.clip(last[i], 0, rows - 1)
        here = pl.ds(pl.multiple_of(row // 16 * 16, 16), 16)
        result = [pltpu.make_async_copy(x.at[here], held.at[i], sems.at[i, 0])]
        at = 0
        for c, wide in enumerate(CHUNKS):
            for j, source in enumerate((mines[c], theirs[c])):
                result.append(
                    pltpu.make_async_copy(
                        source.at[here],
                        terms.at[j, i, :, at : at + wide],
                        sems.at[i, 1 + 2 * c + j],
                    )
                )
            at += wide
        return result

    count = held.shape[0]
    for i in range(count):
        for copy in copies(i):
            copy.start()
    out_ref[...] = jnp.zeros_like(out_ref)
    for i in range(count):
        for copy in copies(i):
            copy.wait()
        summed = held[i].astype(jnp.float32) + (
            terms[0, i].astype(jnp.float32) + terms[1, i].astype(jnp.float32)
        )
        squares = jnp.sum(summed * summed, axis=-1, keepdims=True) / width
        graded = jnp.sum(summed * rating_ref[...].astype(jnp.float32), axis=-1, keepdims=True)
        graded = graded * lax.rsqrt(squares + epsilon)
        place = lax.broadcasted_iota(jnp.int32, graded.shape, 0)
        wanted = (place == last[i] % 16) & (last[i] >= 0) & (last[i] < rows)
        graded = jnp.sum(jnp.where(wanted, graded, 0.0), axis=0, keepdims=True)
        out_ref[i : i + 1, :] = jnp.broadcast_to(graded, (1, out_ref.shape[1]))


def score(half, lengths, rating, x, mines, theirs):
    width = x.shape[1]
    count = lengths.shape[0]
    whole = pl.BlockSpec(memory_space=pltpu.HBM)
    n = 2 * len(mines)
    return pl.pallas_call(
        score_kernel,
        grid_spec=pltpu.PrefetchScalarGridSpec(
            num_scalar_prefetch=2,
            grid=(1,),
            in_specs=[pl.BlockSpec((1, width), lambda i, h, l: (0, 0)), whole] + [whole] * n,
            out_specs=pl.BlockSpec((8, 128), lambda i, h, l: (0, 0)),
            scratch_shapes=[
                pltpu.VMEM((count, 16, width), jnp.bfloat16),
                pltpu.VMEM((2, count, 16, width), jnp.bfloat16),
                pltpu.SemaphoreType.DMA((count, n + 1)),
            ],
        ),
        out_shape=jax.ShapeDtypeStruct((8, 128), jnp.float32),
        compiler_params=pltpu.CompilerParams(vmem_limit_bytes=VMEM),
        cost_estimate=pl.CostEstimate(
            flops=8 * 64 * width, bytes_accessed=6 * 64 * width, transcendentals=0
        ),
        name="score",
    )(half, lengths, rating, x, *mines, *theirs)


def choose_kernel(phase, retained, spread, chosen, held, in_sems, out_sems):
    packs = chosen.shape[0]
    wanted = [retained[jnp.minimum(phase[0], retained.shape[0] - 1), k] for k in range(packs)]

    def fetch(k):
        source = spread.at[jnp.clip(wanted[k], 0, packs - 1)]
        return pltpu.make_async_copy(source, held.at[k], in_sems.at[k])

    def store(k):
        return pltpu.make_async_copy(held.at[k], chosen.at[k], out_sems.at[k])

    for k in range(packs):
        fetch(k).start()
    for k in range(packs):
        fetch(k).wait()

        @pl.when(wanted[k] < 0)
        def _():
            held[k] = jnp.zeros(held.shape[1:], held.dtype)

        store(k).start()
    for k in range(packs):
        store(k).wait()


def choose(phase, retained, spread):
    packs, rows, wide = spread.shape
    return pl.pallas_call(
        choose_kernel,
        grid_spec=pltpu.PrefetchScalarGridSpec(
            num_scalar_prefetch=2,
            grid=(1,),
            in_specs=[pl.BlockSpec(memory_space=pltpu.HBM)],
            out_specs=pl.BlockSpec(memory_space=pltpu.HBM),
            scratch_shapes=[
                pltpu.VMEM((packs, rows, wide), jnp.bfloat16),
                pltpu.SemaphoreType.DMA((packs,)),
                pltpu.SemaphoreType.DMA((packs,)),
            ],
        ),
        out_shape=jax.ShapeDtypeStruct(spread.shape, spread.dtype),
        compiler_params=pltpu.CompilerParams(vmem_limit_bytes=VMEM),
        cost_estimate=pl.CostEstimate(
            flops=0, bytes_accessed=4 * packs * rows * wide, transcendentals=0
        ),
        name="choose",
    )(phase, retained, spread)


def on_device(
    latent_states,
    piece_extents,
    retained_bundles,
    mixer_scaling_factor,
    asker_projector,
    asker_offset_vector,
    lookup_projector,
    content_projector,
    content_offset_vector,
    mixer_output_matrix,
    leave_rating_matrix,
):
    local = latent_states[0, 0, :, 0]
    rows, width = local.shape
    n_dp = lax.axis_size("dp")
    half = lax.axis_index("tensor").astype(jnp.int32).reshape(1)
    phase = lax.axis_index("section").astype(jnp.int32).reshape(1)
    lengths = piece_extents.reshape(piece_extents.shape[-1])
    w_query = asker_projector[0]
    w_key = lookup_projector[0]
    w_value = content_projector[0]
    w_out = mixer_output_matrix[0]
    operands = (
        mixer_scaling_factor,
        asker_offset_vector,
        content_offset_vector,
        w_query,
        w_key,
        w_value,
    )
    other = swap(local)
    qkv = qkv_half(half, lengths, local, *operands, None)
    qkv = qkv_half(1 - half, lengths, other, *operands, qkv)
    mixed = attention(lengths, qkv, w_query.shape[1], w_key.shape[1])

    forward = [(s, s + 1) for s in range(lax.axis_size("section") - 1)]

    def exchange(value):
        return lax.all_to_all(value, "dp", 0, 0)

    def onward(value):
        return lax.ppermute(value, "section", forward)

    mines = []
    theirs = []
    outs = []
    at = 0
    for wide in CHUNKS:
        mine, sent = out_project(half, mixed, w_out, at, wide)
        received = swap(sent)
        mines.append(mine)
        theirs.append(received)
        out = local[:, at : at + wide].astype(jnp.float32) + (
            mine.astype(jnp.float32) + received.astype(jnp.float32)
        )
        outs.append(out.astype(jnp.bfloat16).reshape(n_dp, rows // n_dp, wide))
        at += wide
    first = choose(phase, retained_bundles, exchange(outs[0]))
    moved = onward(first)
    first, second = lax.optimization_barrier((first, outs[1]))
    second = exchange(choose(phase, retained_bundles, exchange(second)))
    second, moved = lax.optimization_barrier((second, moved))
    second = onward(second)
    first = exchange(moved)
    arrived = [v.reshape(rows, v.shape[2]) for v in (first, second)]
    scores = score(half, lengths, leave_rating_matrix, local, mines, theirs)
    scores = scores[: lengths.shape[0], 0]
    seg_scores = lax.psum(scores, "tensor")
    arrived = jnp.concatenate(arrived, axis=1)
    return (seg_scores[None, None, None], arrived[None, None, :, None, :])


def solution(mesh):
    return jax.shard_map(
        on_device,
        mesh=mesh,
        in_specs=(
            P("section", "dp", "tensor", None, None),
            P("section", "dp", None, None),
            P(),
            P("section", None),
            P("section", None, "tensor"),
            P("section", "tensor"),
            P("section", None, "tensor"),
            P("section", None, "tensor"),
            P("section", "tensor"),
            P("section", "tensor", None),
            P("section", None),
        ),
        out_specs=(P("section", "dp", None, None), P("section", "dp", "tensor", None, None)),
        check_vma=False,
    )
```

time: 249 us -> 179 us (0.72)
  Pallas kernels: 0 us -> 67.6 us
  matrix products: 47.5 us -> 0 us
  blocking collectives: 31.6 us -> 2.97 us
  local copies, waits for them, and re-layouts: 32.5 us -> 4.24 us
  other arithmetic: 33 us -> 8.58 us
  waiting for transfers between devices: 81.8 us -> 69.3 us
  starting transfers between devices: 20.9 us -> 24.8 us
    pallas_call x0 -> x8, Pallas kernels: none -> 67.6 us  [the longest x2 28.7 us: qkv_half(): pl.pallas_call(qkv_kernel, grid_spec=pltpu.PrefetchScalarGridSpec(num_sca...]
    dot_general x7 -> x0, matrix products: 47.5 us -> none  [the longest x2 13.3 us: on_device(): jnp.dot(mixed, w_out[:, span], preferred_element_type=jnp.float32)]
    all_to_all x1 -> x0, blocking collectives: 28.6 us -> none  [on_device(): spread = lax.all_to_all(out, 'dp', 0, 0)]
    ppermute x2, waiting for transfers between devices: 47 us -> 27.4 us  [onward(): return lax.ppermute(value, 'section', forward)]
    all_to_all x3 -> x4, waiting for transfers between devices: 31.1 us -> 41.9 us  [exchange(): return lax.all_to_all(value, 'dp', 0, 0)]
    sub x2 -> x0, other arithmetic: 8.21 us -> none  [the longest x1 8.21 us: on_device(): expons = jnp.exp(logits - peak)]
    dot_general x1 -> x0, local copies, waits for them, and re-layouts: 7.88 us -> none  [on_device(): keys = jnp.dot(piece, w_key, preferred_element_type=jnp.float32)]
    select_n x2 -> x0, other arithmetic: 6.46 us -> none  [the longest x1 3.31 us: on_device(): first = jnp.where(tensor == 0, normed, other)]
  transfers between devices with their start and end apart: 8 -> 9, of which waited for: 6 -> 5; matrix products, arithmetic and copies ran while one was open for 7% -> 4% of each run, Pallas kernels for 0% -> 17%
where the time goes in v2:
time: 179 us; the launch traced here: 178 us
  waiting for transfers between devices  69.3 us (39%)
  Pallas kernels  67.6 us (38%)
  starting transfers between devices  24.8 us (14%)
  other arithmetic  8.58 us (5%)
  local copies, waits for them, and re-layouts  4.24 us (2%)
  blocking collectives  2.97 us (2%)
    all_to_all x4, waiting for transfers between devices, exchange(): return lax.all_to_all(value, 'dp', 0, 0)  41.9 us
    pallas_call x2, Pallas kernels, qkv_half(): pl.pallas_call(qkv_kernel, grid_spec=pltpu.PrefetchScalarGridSpec(num_sca...  28.7 us
    ppermute x2, waiting for transfers between devices, onward(): return lax.ppermute(value, 'section', forward)  27.4 us
    pallas_call x2, Pallas kernels, out_project(): pl.pallas_call(functools.partial(out_kernel, at), grid_spec=pltpu.Prefetc...  19.5 us
    all_to_all x4, starting transfers between devices, exchange(): return lax.all_to_all(value, 'dp', 0, 0)  19.1 us
    pallas_call x1, Pallas kernels, attention(): pl.pallas_call(attention_kernel, grid_spec=pltpu.PrefetchScalarGridSpec(n...  8.3 us
    pallas_call x2, Pallas kernels, choose(): pl.pallas_call(choose_kernel, grid_spec=pltpu.PrefetchScalarGridSpec(num_...  7.12 us
    convert_element_type x2, other arithmetic, on_device(): outs.append(out.astype(jnp.bfloat16).reshape(n_dp, rows // n_dp, wide))  6.89 us
  transfers between devices with their start and end apart: 9, of which 5 were waited for; matrix products, arithmetic and copies ran while one was open for 4% of the time, Pallas kernels for 17%

profile of v2, /device:TPU:2, one launch (start us, length us, event | category | flops | bytes accessed | tf_op | source)
XLA Modules:
  0.0 178.3 jit_solution(11448039207125559664)
XLA Ops:
  0.6 0.1 collective-permute-start
  0.7 14.2 %qkv.2.rest_0_ = bf16[512,2560]{1,0:T(8,128)(2,1)} custom-call(s32[1]{0:T(128)} %bitcast.half, s32[4]{0:T(128)} %bitcast.31, bf16[1,5120]{1,0:T(2,128)(2,1)} %gain_ref.3, bf16[1,1536]{1,0:T(2,128)(2,1)} %q_bias_ref.3, bf16[1,512]{1,0:T(2,128)(2,1)} %v_bias_ref.3, bf16[256,5120]{1,0:T(8,128)(2,1)} %bitcast.18, bf16[5120,1536]{1,0:T(8,128)(2,1)} %bitcast.15, ...), custom_call_target="tpu_custom_call" | custom-call | flops 6710886400 | bytes 26214400 | tf_op jit(solution)/shard_map/qkv/pallas_call | solution.py:141
  15.0 0.0 copy-start.2
  15.0 1.5 copy-done.2
  16.5 14.5 %qkv.3.q_ref.k_ref.v_ref = bf16[512,2560]{1,0:T(8,128)(2,1)} custom-call(s32[1]{0:T(128)S(6)} %sub.3.half, s32[4]{0:T(128)} %bitcast.32, bf16[1,5120]{1,0:T(2,128)(2,1)} %gain_ref.3, bf16[1,1536]{1,0:T(2,128)(2,1)} %q_bias_ref.3, bf16[1,512]{1,0:T(2,128)(2,1)} %v_bias_ref.3, bf16[256,5120]{1,0:T(8,128)(2,1)} %copy-done.2, ...), custom_call_target="tpu_custom_call", output_to_operand_aliasing={{}: (9, {})} | custom-call | flops 6710886400 | bytes 26214400 | tf_op jit(solution)/shard_map/qkv/pallas_call | solution.py:141
  30.9 8.3 %attention.1.mixed = bf16[512,1536]{1,0:T(8,128)(2,1)} custom-call(s32[4]{0:T(128)} %bitcast.33, bf16[512,2560]{1,0:T(8,128)(2,1)} %qkv.3.q_ref.k_ref.v_ref, bf16[512,2560]{1,0:T(8,128)(2,1)} %qkv.3.q_ref.k_ref.v_ref, bf16[512,2560]{1,0:T(8,128)(2,1)} %qkv.3.q_ref.k_ref.v_ref), custom_call_target="tpu_custom_call" | custom-call | flops 3221225472 | bytes 6291456 | tf_op jit(solution)/shard_map/attention/pallas_call | solution.py:209
  39.2 11.2 %out_project.2 = (bf16[256,3072]{1,0:T(8,128)(2,1)}, bf16[256,3072]{1,0:T(8,128)(2,1)}) custom-call(s32[1]{0:T(128)} %bitcast.half, bf16[512,1536]{1,0:T(8,128)(2,1)} %attention.1.mixed, bf16[1536,5120]{1,0:T(8,128)(2,1)} %bitcast.26), custom_call_target="tpu_custom_call" | custom-call | flops 4831838208 | bytes 9437184 | tf_op jit(solution)/shard_map/out_project/pallas_call | solution.py:288
  50.4 0.0 copy-start
  50.4 0.6 collective-permute-start.1
  51.0 8.3 %out_project.3 = (bf16[256,2048]{1,0:T(8,128)(2,1)}, bf16[256,2048]{1,0:T(8,128)(2,1)}) custom-call(s32[1]{0:T(128)} %bitcast.half, bf16[512,1536]{1,0:T(8,128)(2,1)} %attention.1.mixed, bf16[1536,5120]{1,0:T(8,128)(2,1)} %bitcast.27), custom_call_target="tpu_custom_call" | custom-call | flops 3221225472 | bytes 6291456 | tf_op jit(solution)/shard_map/out_project/pallas_call | solution.py:288
  59.3 0.1 collective-permute-start.2
  59.4 3.8 %add_convert_fusion = bf16[256,3072]{1,0:T(8,128)(2,1)} fusion(bf16[256,3072]{1,0:T(8,128)(2,1)} %collective-permute-done.1.rest_2_, bf16[256,3072]{1,0:T(8,128)(2,1)} %get-tuple-element.9.rest_0_, bf16[256,5120]{1,0:T(8,128)(2,1)S(1)} %bitcast.20), kind=kLoop, calls=%fused_computation | loop fusion | flops 4718592 | bytes 6291456 | tf_op jit(solution)/shard_map/convert_element_type | solution.py:490
  63.2 8.1 %all-to-all-start = ((bf16[16,16,3072]{2,1,0:T(8,128)(2,1)}), bf16[16,16,3072]{2,1,0:T(8,128)(2,1)}, u32[]{:S(2)}, u32[]{:S(2)}) async-start(bf16[16,16,3072]{2,1,0:T(8,128)(2,1)} %bitcast.29), calls=%async_computation | async-start | bytes 3145728 | tf_op jit(solution)/shard_map/all_to_all | solution.py:473
  71.3 3.1 %add_convert_fusion.1 = bf16[256,2048]{1,0:T(8,128)(2,1)} fusion(bf16[256,2048]{1,0:T(8,128)(2,1)} %collective-permute-done.2.rest_3_, bf16[256,2048]{1,0:T(8,128)(2,1)} %get-tuple-element.10.rest_1_, bf16[256,5120]{1,0:T(8,128)(2,1)S(1)} %bitcast.21), kind=kLoop, calls=%fused_computation.2 | loop fusion | flops 3145728 | bytes 4194304 | tf_op jit(solution)/shard_map/convert_element_type | solution.py:490
  74.4 23.4 %all-to-all-done.spread = bf16[16,16,3072]{2,1,0:T(8,128)(2,1)} async-done(((bf16[16,16,3072]{2,1,0:T(8,128)(2,1)}), bf16[16,16,3072]{2,1,0:T(8,128)(2,1)}, u32[]{:S(2)}, u32[]{:S(2)}) %all-to-all-start) | async-done | bytes 1572896 | tf_op jit(solution)/shard_map/all_to_all | solution.py:473
  97.8 3.8 %choose.2 = bf16[16,16,3072]{2,1,0:T(8,128)(2,1)} custom-call(s32[1]{0:T(128)} %bitcast.7.phase, s32[3,16]{1,0:T(4,128)} %retained.3, bf16[16,16,3072]{2,1,0:T(8,128)(2,1)} %all-to-all-done.spread), custom_call_target="tpu_custom_call" | custom-call | bytes 3145728 | tf_op jit(solution)/shard_map/choose/pallas_call | solution.py:412
  101.6 3.7 %all-to-all-start.1 = ((bf16[16,16,2048]{2,1,0:T(8,128)(2,1)}), bf16[16,16,2048]{2,1,0:T(8,128)(2,1)S(1)}, u32[]{:S(2)}, u32[]{:S(2)}) async-start(bf16[16,16,2048]{2,1,0:T(8,128)(2,1)} %bitcast.9), calls=%async_computation.1 | async-start | bytes 2097152 | tf_op jit(solution)/shard_map/all_to_all | solution.py:473
  105.3 2.7 %collective-permute-start.3 = (bf16[16,16,3072]{2,1,0:T(8,128)(2,1)}, bf16[16,16,3072]{2,1,0:T(8,128)(2,1)}, u32[]{:S(2)}, u32[]{:S(2)}) collective-permute-start(bf16[16,16,3072]{2,1,0:T(8,128)(2,1)} %choose.2), channel_id=1, source_target_pairs={{0,32},{32,64},{64,96},{1,33},{33,65},{65,97},{2,34},{34,66},{66,9... | collective-permute-start | bytes 4718600 | tf_op jit(solution)/shard_map/ppermute | solution.py:476
  108.0 14.7 %all-to-all-done.1.spread = bf16[16,16,2048]{2,1,0:T(8,128)(2,1)S(1)} async-done(((bf16[16,16,2048]{2,1,0:T(8,128)(2,1)}), bf16[16,16,2048]{2,1,0:T(8,128)(2,1)S(1)}, u32[]{:S(2)}, u32[]{:S(2)}) %all-to-all-start.1) | async-done | bytes 1048608 | tf_op jit(solution)/shard_map/all_to_all | solution.py:473
  122.7 1.0 copy-done.1
  123.7 3.3 %choose.3 = bf16[16,16,2048]{2,1,0:T(8,128)(2,1)} custom-call(s32[1]{0:T(128)} %bitcast.7.phase, s32[3,16]{1,0:T(4,128)} %retained.3, bf16[16,16,2048]{2,1,0:T(8,128)(2,1)} %copy-done.1), custom_call_target="tpu_custom_call" | custom-call | bytes 2097152 | tf_op jit(solution)/shard_map/choose/pallas_call | solution.py:412
  127.0 3.7 %all-to-all-start.2 = ((bf16[16,16,2048]{2,1,0:T(8,128)(2,1)}), bf16[16,16,2048]{2,1,0:T(8,128)(2,1)S(1)}, u32[]{:S(2)}, u32[]{:S(2)}) async-start(bf16[16,16,2048]{2,1,0:T(8,128)(2,1)} %choose.3), calls=%async_computation.2 | async-start | bytes 2097152 | tf_op jit(solution)/shard_map/all_to_all | solution.py:473
  130.7 12.5 %collective-permute-done.3 = bf16[16,16,3072]{2,1,0:T(8,128)(2,1)} collective-permute-done((bf16[16,16,3072]{2,1,0:T(8,128)(2,1)}, bf16[16,16,3072]{2,1,0:T(8,128)(2,1)}, u32[]{:S(2)}, u32[]{:S(2)}) %collective-permute-start.3) | collective-permute-done | bytes 1572896 | tf_op jit(solution)/shard_map/ppermute | solution.py:476
  143.2 3.8 %all-to-all-done.2 = bf16[16,16,2048]{2,1,0:T(8,128)(2,1)S(1)} async-done(((bf16[16,16,2048]{2,1,0:T(8,128)(2,1)}), bf16[16,16,2048]{2,1,0:T(8,128)(2,1)S(1)}, u32[]{:S(2)}, u32[]{:S(2)}) %all-to-all-start.2) | async-done | bytes 1048608 | tf_op jit(solution)/shard_map/all_to_all | solution.py:473
  146.9 1.0 copy-done.3
  147.9 3.7 %all-to-all-start.3 = ((bf16[16,16,3072]{2,1,0:T(8,128)(2,1)}), bf16[16,16,3072]{2,1,0:T(8,128)(2,1)S(1)}, u32[]{:S(2)}, u32[]{:S(2)}) async-start(bf16[16,16,3072]{2,1,0:T(8,128)(2,1)} %collective-permute-done.3), calls=%async_computation.3 | async-start | bytes 3145728 | tf_op jit(solution)/shard_map/all_to_all | solution.py:473
  151.6 2.3 %collective-permute-start.4 = (bf16[16,16,2048]{2,1,0:T(8,128)(2,1)}, bf16[16,16,2048]{2,1,0:T(8,128)(2,1)S(1)}, u32[]{:S(2)}, u32[]{:S(2)}) collective-permute-start(bf16[16,16,2048]{2,1,0:T(8,128)(2,1)} %copy-done.3), channel_id=1, source_target_pairs={{0,32},{32,64},{64,96},{1,33},{33,65},{65,97},{2,34},{34,66},{66,9... | collective-permute-start | bytes 3145736 | tf_op jit(solution)/shard_map/ppermute | solution.py:476
  153.9 4.1 %score.1 = f32[8,128]{1,0:T(8,128)} custom-call(s32[1]{0:T(128)} %bitcast.half, s32[4]{0:T(128)} %bitcast.34, bf16[1,5120]{1,0:T(2,128)(2,1)} %rating_ref.1, bf16[256,5120]{1,0:T(8,128)(2,1)} %bitcast.19, bf16[256,3072]{1,0:T(8,128)(2,1)} %get-tuple-element.9.rest_0_, bf16[256,2048]{1,0:T(8,128)(2,1)} %get-tuple-element.10.rest_1_, ...), custom_call_target="tpu_custom_call" | custom-call | flops 2621440 | bytes 1966080 | tf_op jit(solution)/shard_map/score/pallas_call | solution.py:363
  158.0 0.8 slice_reduce_fusion
  158.8 3.0 %psum.7 = f32[1,1,1,4]{3,2,1,0:T(1,128)} all-reduce(f32[1,1,1,4]{3,2,1,0:T(1,128)S(1)} %bitcast.35), channel_id=1, replica_groups=mesh['section'=4,'dp'=16,'tensor'=2] {'tensor'}, use_global_device_ids=true, to_apply=%region_0.0 | all-reduce | flops 4 | bytes 32 | tf_op jit(solution)/shard_map/psum | solution.py:502
  161.7 14.9 %collective-permute-done.4 = bf16[16,16,2048]{2,1,0:T(8,128)(2,1)S(1)} collective-permute-done((bf16[16,16,2048]{2,1,0:T(8,128)(2,1)}, bf16[16,16,2048]{2,1,0:T(8,128)(2,1)S(1)}, u32[]{:S(2)}, u32[]{:S(2)}) %collective-permute-start.4) | collective-permute-done | bytes 1048608 | tf_op jit(solution)/shard_map/ppermute | solution.py:476
  176.6 1.7 maximum_bitcast_fusion
  (7 shorter events, 0.0 us)
Async XLA Ops:
  0.6 14.3 %collective-permute-start = (bf16[256,5120]{1,0:T(8,128)(2,1)}, bf16[256,5120]{1,0:T(8,128)(2,1)S(1)}, u32[]{:S(2)}, u32[]{:S(2)}) collective-permute-start(bf16[256,5120]{1,0:T(8,128)(2,1)} %bitcast.17), channel_id=1, source_target_pairs={{0,1},{1,0},{2,3},{3,2},{4,5},{5,4},{6,7},{7,6},{8,9},{9,8},{10,11... | collective-permute-start | bytes 7864328 | tf_op jit(solution)/shard_map/ppermute | solution.py:36
  15.0 1.5 copy-start.2
  50.4 9.0 %copy-start = (bf16[1,1,256,1,5120]{4,2,3,1,0:T(8,128)(2,1)S(1)}, bf16[1,1,256,1,5120]{4,2,3,1,0:T(8,128)(2,1)}, u32[]{:S(2)}) copy-start(bf16[1,1,256,1,5120]{4,2,3,1,0:T(8,128)(2,1)} %param.11) | copy-start | bytes 7864324
  50.4 8.9 %collective-permute-start.1 = (bf16[256,3072]{1,0:T(8,128)(2,1)}, bf16[256,3072]{1,0:T(8,128)(2,1)}, u32[]{:S(2)}, u32[]{:S(2)}) collective-permute-start(bf16[256,3072]{1,0:T(8,128)(2,1)} %get-tuple-element.11), channel_id=1, source_target_pairs={{0,1},{1,0},{2,3},{3,2},{4,5},{5,4},{6,7},{7,6},{8,9},{9,8},{10,11... | collective-permute-start | bytes 4718600 | tf_op jit(solution)/shard_map/ppermute | solution.py:36
  59.3 12.0 %collective-permute-start.2 = (bf16[256,2048]{1,0:T(8,128)(2,1)}, bf16[256,2048]{1,0:T(8,128)(2,1)}, u32[]{:S(2)}, u32[]{:S(2)}) collective-permute-start(bf16[256,2048]{1,0:T(8,128)(2,1)} %get-tuple-element.12), channel_id=1, source_target_pairs={{0,1},{1,0},{2,3},{3,2},{4,5},{5,4},{6,7},{7,6},{8,9},{9,8},{10,11... | collective-permute-start | bytes 3145736 | tf_op jit(solution)/shard_map/ppermute | solution.py:36
  63.2 34.6 %all-to-all-start = ((bf16[16,16,3072]{2,1,0:T(8,128)(2,1)}), bf16[16,16,3072]{2,1,0:T(8,128)(2,1)}, u32[]{:S(2)}, u32[]{:S(2)}) async-start(bf16[16,16,3072]{2,1,0:T(8,128)(2,1)} %bitcast.29), calls=%async_computation | async-start | bytes 3145728 | tf_op jit(solution)/shard_map/all_to_all | solution.py:473
  101.6 21.1 %all-to-all-start.1 = ((bf16[16,16,2048]{2,1,0:T(8,128)(2,1)}), bf16[16,16,2048]{2,1,0:T(8,128)(2,1)S(1)}, u32[]{:S(2)}, u32[]{:S(2)}) async-start(bf16[16,16,2048]{2,1,0:T(8,128)(2,1)} %bitcast.9), calls=%async_computation.1 | async-start | bytes 2097152 | tf_op jit(solution)/shard_map/all_to_all | solution.py:473
  105.3 37.9 %collective-permute-start.3 = (bf16[16,16,3072]{2,1,0:T(8,128)(2,1)}, bf16[16,16,3072]{2,1,0:T(8,128)(2,1)}, u32[]{:S(2)}, u32[]{:S(2)}) collective-permute-start(bf16[16,16,3072]{2,1,0:T(8,128)(2,1)} %choose.2), channel_id=1, source_target_pairs={{0,32},{32,64},{64,96},{1,33},{33,65},{65,97},{2,34},{34,66},{66,9... | collective-permute-start | bytes 4718600 | tf_op jit(solution)/shard_map/ppermute | solution.py:476
  122.7 1.0 copy-start.1
  127.0 19.9 %all-to-all-start.2 = ((bf16[16,16,2048]{2,1,0:T(8,128)(2,1)}), bf16[16,16,2048]{2,1,0:T(8,128)(2,1)S(1)}, u32[]{:S(2)}, u32[]{:S(2)}) async-start(bf16[16,16,2048]{2,1,0:T(8,128)(2,1)} %choose.3), calls=%async_computation.2 | async-start | bytes 2097152 | tf_op jit(solution)/shard_map/all_to_all | solution.py:473
  146.9 1.0 copy-start.3
  147.9 28.7 %all-to-all-start.3 = ((bf16[16,16,3072]{2,1,0:T(8,128)(2,1)}), bf16[16,16,3072]{2,1,0:T(8,128)(2,1)S(1)}, u32[]{:S(2)}, u32[]{:S(2)}) async-start(bf16[16,16,3072]{2,1,0:T(8,128)(2,1)} %collective-permute-done.3), calls=%async_computation.3 | async-start | bytes 3145728 | tf_op jit(solution)/shard_map/all_to_all | solution.py:473
  151.6 25.0 %collective-permute-start.4 = (bf16[16,16,2048]{2,1,0:T(8,128)(2,1)}, bf16[16,16,2048]{2,1,0:T(8,128)(2,1)S(1)}, u32[]{:S(2)}, u32[]{:S(2)}) collective-permute-start(bf16[16,16,2048]{2,1,0:T(8,128)(2,1)} %copy-done.3), channel_id=1, source_target_pairs={{0,32},{32,64},{64,96},{1,33},{33,65},{65,97},{2,34},{34,66},{66,9... | collective-permute-start | bytes 3145736 | tf_op jit(solution)/shard_map/ppermute | solution.py:476

commit v3 on v2

v3 whole, which is shorter than its diff:
```python
import functools
import jax
import jax.numpy as jnp
from jax import lax
from jax.experimental import pallas as pl
from jax.experimental.pallas import tpu as pltpu
from jax.sharding import PartitionSpec as P

HD = 128
TILE = 512
AHEAD = 8
CHUNKS = (2560, 2560)
VMEM = 60 * 1024 * 1024
COST = pl.CostEstimate(flops=1, bytes_accessed=1, transcendentals=0)

epsilon = 1e-06
rope_base = 1000000.0


def ends_of(lengths):
    ends = []
    total = 0
    for i in range(lengths.shape[0]):
        total = total + lengths[i]
        ends.append(total)
    return ends


def starts_at(places, ends):
    start = jnp.zeros_like(places)
    for end in ends[:-1]:
        start = jnp.where(places >= end, end, start)
    return start


def swap(value):
    return lax.ppermute(value, "tensor", [(0, 1), (1, 0)])


def qkv_kernel(half, lengths, gain_ref, q_bias_ref, v_bias_ref, x, other, wq, wk, wv, *rest):
    out, held, normed, weights, ready, turns, x_sems, w_sems, out_sems = rest
    rows, width = normed.shape
    few = rows // 8
    slots, deep = weights.shape[:2]
    tiles = []
    for source in (wq, wk, wv):
        for at in range(0, source.shape[1], TILE):
            tiles.append((source, at))
    n_query = wq.shape[1] // TILE
    n_rope = n_query + wk.shape[1] // TILE
    parts = width // deep
    total = len(tiles) * parts

    def x_copy(r):
        source = (x, other)[r // 4]
        here = source.at[r % 4 * few : (r % 4 + 1) * few]
        return pltpu.make_async_copy(here, held.at[r * few : (r + 1) * few], x_sems.at[r])

    def w_copy(j):
        source, at = tiles[j // parts]
        d = j % parts
        return pltpu.make_async_copy(
            source.at[d * deep : (d + 1) * deep, at : at + TILE],
            weights.at[j % slots],
            w_sems.at[j % slots],
        )

    def out_copy(t):
        return pltpu.make_async_copy(
            ready.at[:, t * TILE : (t + 1) * TILE],
            out.at[:, t * TILE : (t + 1) * TILE],
            out_sems.at[t],
        )

    for r in range(8):
        x_copy(r).start()
    for j in range(parts):
        w_copy(j).start()
    places = lax.broadcasted_iota(jnp.int32, (rows, HD), 0)
    offset = (places - starts_at(places, ends_of(lengths))).astype(jnp.float32)
    lane = lax.broadcasted_iota(jnp.int32, (1, HD), 1)
    order = (lane % (HD // 2)).astype(jnp.float32) * 2.0
    angle = offset * jnp.exp(-jnp.log(rope_base) * order / HD)
    turns[0] = jnp.cos(angle)
    turns[1] = jnp.where(lane < HD // 2, -1.0, 1.0) * jnp.sin(angle)
    for r in range(8):
        x_copy(r).wait()
        if r == 4:
            for j in range(parts, AHEAD):
                w_copy(j).start()
        shift = (r // 4 + half[0]) % 2 * (rows // 2) + r % 4 * few
        for at in range(0, few, 16):
            v = held[r * few + at : r * few + at + 16, :].astype(jnp.float32)
            factor = lax.rsqrt(jnp.mean(v * v, axis=-1, keepdims=True) + epsilon)
            normed[pl.ds(pl.multiple_of(shift + at, 16), 16), :] = (
                v * factor * gain_ref[...].astype(jnp.float32)
            ).astype(jnp.bfloat16)

    for t in range(len(tiles)):
        for d in range(parts):
            w_copy(t * parts + d).wait()
        for j in range(t * parts + AHEAD, min((t + 1) * parts + AHEAD, total)):
            w_copy(j).start()
        part = None
        for d in range(parts):
            term = jnp.dot(
                normed[:, d * deep : (d + 1) * deep],
                weights[(t * parts + d) % slots],
                preferred_element_type=jnp.float32,
            )
            part = term if part is None else part + term
        here = slice(t * TILE, (t + 1) * TILE)
        if t < n_query:
            part = part + q_bias_ref[:, here].astype(jnp.float32)
        elif t >= n_rope:
            there = slice((t - n_rope) * TILE, (t - n_rope + 1) * TILE)
            part = part + v_bias_ref[:, there].astype(jnp.float32)
        if t < n_rope:
            for at in range(0, TILE, HD):
                u = part[:, at : at + HD]
                turned = u * turns[0] + pltpu.roll(u, HD // 2, 1) * turns[1]
                ready[:, t * TILE + at : t * TILE + at + HD] = turned.astype(jnp.bfloat16)
        else:
            ready[:, here] = part.astype(jnp.bfloat16)
        out_copy(t).start()
    for t in range(len(tiles)):
        out_copy(t).wait()


def project_in(half, lengths, x, other, gain, q_bias, v_bias, wq, wk, wv):
    rows, width = 2 * x.shape[0], x.shape[1]
    columns = wq.shape[1] + wk.shape[1] + wv.shape[1]
    n = columns // TILE
    whole = pl.BlockSpec(memory_space=pltpu.HBM)
    operands = [gain, q_bias, v_bias, x, other, wq, wk, wv]
    specs = [pl.BlockSpec(v.shape, lambda i, h, l: (0, 0)) for v in operands[:3]] + [whole] * 5
    return pl.pallas_call(
        qkv_kernel,
        grid_spec=pltpu.PrefetchScalarGridSpec(
            num_scalar_prefetch=2,
            grid=(1,),
            in_specs=specs,
            out_specs=whole,
            scratch_shapes=[
                pltpu.VMEM((rows, width), jnp.bfloat16),
                pltpu.VMEM((rows, width), jnp.bfloat16),
                pltpu.VMEM((AHEAD + 5, width // 5, TILE), jnp.bfloat16),
                pltpu.VMEM((rows, columns), jnp.bfloat16),
                pltpu.VMEM((2, rows, HD), jnp.float32),
                pltpu.SemaphoreType.DMA((8,)),
                pltpu.SemaphoreType.DMA((AHEAD + 5,)),
                pltpu.SemaphoreType.DMA((n,)),
            ],
        ),
        out_shape=jax.ShapeDtypeStruct((rows, columns), jnp.bfloat16),
        compiler_params=pltpu.CompilerParams(vmem_limit_bytes=VMEM),
        cost_estimate=COST,
        name="qkv",
    )(half, lengths, *operands)


def attention_kernel(half, lengths, q_ref, k_ref, v_ref, out_ref):
    ends = ends_of(lengths)
    rows = q_ref.shape[0]
    groups = k_ref.shape[1] // HD
    heads = q_ref.shape[1] // HD // groups
    block = 128

    def rows_of(first):
        for i in range(0, rows, block):
            hi = first + i + block
            lo = max(0, hi - 3 * block)
            here = slice(i, i + block)
            b = lo + lax.broadcasted_iota(jnp.int32, (hi - lo, block), 0)
            a = hi - block + lax.broadcasted_iota(jnp.int32, (hi - lo, block), 1)
            start = starts_at(hi - block + lax.broadcasted_iota(jnp.int32, (1, block), 1), ends)
            allowed = (b <= a) & (b >= start)
            allowed = jnp.concatenate([allowed] * heads, axis=1)
            for g in range(groups):
                at = slice(g * HD, (g + 1) * HD)
                places = [slice(h * HD, (h + 1) * HD) for h in range(g * heads, (g + 1) * heads)]
                q = jnp.concatenate([q_ref[here, place] for place in places], axis=0)
                logits = lax.dot_general(
                    k_ref[lo:hi, at],
                    q,
                    (((1,), (1,)), ((), ())),
                    preferred_element_type=jnp.float32,
                ) * HD ** (-0.5)
                logits = jnp.where(allowed, logits, -1e30)
                expons = jnp.exp(logits - jnp.max(logits, axis=0, keepdims=True))
                probs = expons * (1.0 / jnp.sum(expons, axis=0, keepdims=True))
                mixed = lax.dot_general(
                    probs.astype(jnp.bfloat16),
                    v_ref[lo:hi, at],
                    (((0,), (0,)), ((), ())),
                    preferred_element_type=jnp.float32,
                ).astype(jnp.bfloat16)
                for h, place in enumerate(places):
                    out_ref[here, place] = mixed[h * block : (h + 1) * block]

    @pl.when(half[0] == 0)
    def _():
        rows_of(0)

    @pl.when(half[0] != 0)
    def _():
        rows_of(rows)


def attention(half, lengths, qkv, q_width, k_width):
    length = qkv.shape[0]
    rows = length // 2
    pace = 2
    steps = k_width // HD // pace
    wide = q_width // steps
    deep = k_width // steps
    return pl.pallas_call(
        attention_kernel,
        grid_spec=pltpu.PrefetchScalarGridSpec(
            num_scalar_prefetch=2,
            grid=(steps,),
            in_specs=[
                pl.BlockSpec((rows, wide), lambda g, h, l: (h[0], g)),
                pl.BlockSpec((length, deep), lambda g, h, l: (0, q_width // deep + g)),
                pl.BlockSpec((length, deep), lambda g, h, l: (0, (q_width + k_width) // deep + g)),
            ],
            out_specs=pl.BlockSpec((rows, wide), lambda g, h, l: (0, g)),
        ),
        out_shape=jax.ShapeDtypeStruct((rows, q_width), jnp.bfloat16),
        compiler_params=pltpu.CompilerParams(vmem_limit_bytes=VMEM),
        cost_estimate=COST,
        name="attention",
    )(half, lengths, qkv, qkv, qkv)


def choose_kernel(phase, retained, spread, chosen, held, in_sems, out_sems):
    packs, few, _ = spread.shape
    wanted = [retained[jnp.minimum(phase[0], retained.shape[0] - 1), k] for k in range(packs)]

    def fetch(k):
        source = spread.at[jnp.clip(wanted[k], 0, packs - 1)]
        return pltpu.make_async_copy(source, held.at[k * few : (k + 1) * few], in_sems.at[k])

    def store(k):
        here = slice(k * few, (k + 1) * few)
        return pltpu.make_async_copy(held.at[here], chosen.at[here], out_sems.at[k])

    for k in range(packs):
        fetch(k).start()
    for k in range(packs):
        fetch(k).wait()

        @pl.when(wanted[k] < 0)
        def _():
            held[k * few : (k + 1) * few, :] = jnp.zeros((few, held.shape[1]), held.dtype)

        store(k).start()
    for k in range(packs):
        store(k).wait()


def choose(phase, retained, spread):
    packs, few, wide = spread.shape
    whole = pl.BlockSpec(memory_space=pltpu.HBM)
    return pl.pallas_call(
        choose_kernel,
        grid_spec=pltpu.PrefetchScalarGridSpec(
            num_scalar_prefetch=2,
            grid=(1,),
            in_specs=[whole],
            out_specs=whole,
            scratch_shapes=[
                pltpu.VMEM((packs * few, wide), jnp.bfloat16),
                pltpu.SemaphoreType.DMA((packs,)),
                pltpu.SemaphoreType.DMA((packs,)),
            ],
        ),
        out_shape=jax.ShapeDtypeStruct((packs * few, wide), spread.dtype),
        compiler_params=pltpu.CompilerParams(vmem_limit_bytes=VMEM),
        cost_estimate=COST,
        name="choose",
    )(phase, retained, spread)


def out_kernel(at, phase, retained, mixed, latent, w_mine, w_theirs, out, *rest):
    held, latents, weights, ready, m_sems, l_sem, w_sems, out_sems = rest[-8:]
    rows, wide = out.shape
    width = held.shape[1]
    depth = width // 2
    n = wide // TILE

    def w_copies(t):
        here = slice(at + t * TILE, at + (t + 1) * TILE)
        return [
            pltpu.make_async_copy(source.at[:, here], weights.at[t, i], w_sems.at[t, i])
            for i, source in enumerate((w_mine, w_theirs))
        ]

    def out_copy(t):
        here = slice(t * TILE, (t + 1) * TILE)
        return pltpu.make_async_copy(ready.at[:, here], out.at[:, here], out_sems.at[t])

    l_copy = pltpu.make_async_copy(latent.at[:, at : at + wide], latents, l_sem.at[0])
    if at == 0:
        packs, few, _ = mixed.shape
        wanted = [retained[jnp.minimum(phase[0], retained.shape[0] - 1), k] for k in range(packs)]

        def m_copy(k):
            source = mixed.at[jnp.clip(wanted[k], 0, packs - 1)]
            return pltpu.make_async_copy(source, held.at[k * few : (k + 1) * few], m_sems.at[k])

        for copy in w_copies(0):
            copy.start()
        for k in range(packs):
            m_copy(k).start()
        l_copy.start()
        for k in range(packs):
            m_copy(k).wait()

            @pl.when(wanted[k] < 0)
            def _():
                held[k * few : (k + 1) * few, :] = jnp.zeros((few, width), held.dtype)

        keep = pltpu.make_async_copy(held, rest[0], m_sems.at[0])
        keep.start()
    else:
        m_copy = pltpu.make_async_copy(mixed, held, m_sems.at[0])
        m_copy.start()
        for copy in w_copies(0):
            copy.start()
        l_copy.start()
        m_copy.wait()
    for copy in w_copies(1):
        copy.start()
    for t in range(n):
        for copy in w_copies(t):
            copy.wait()
        if t + 2 < n:
            for copy in w_copies(t + 2):
                copy.start()
        here = slice(t * TILE, (t + 1) * TILE)
        branch = 0.0
        for i in range(2):
            term = jnp.dot(
                held[:, i * depth : (i + 1) * depth],
                weights[t, i],
                preferred_element_type=jnp.float32,
            )
            branch = branch + term.astype(jnp.bfloat16).astype(jnp.float32)
        if t == 0:
            l_copy.wait()
        ready[:, here] = (latents[:, here].astype(jnp.float32) + branch).astype(jnp.bfloat16)
        out_copy(t).start()
    for t in range(n):
        out_copy(t).wait()
    if at == 0:
        keep.wait()


def out_project(phase, retained, mixed, latent, w_mine, w_theirs, at, wide):
    rows = latent.shape[0]
    width = mixed.shape[-1]
    n = wide // TILE
    whole = pl.BlockSpec(memory_space=pltpu.HBM)
    result = [jax.ShapeDtypeStruct((rows, wide), jnp.bfloat16)]
    if at == 0:
        result.append(jax.ShapeDtypeStruct((rows, width), jnp.bfloat16))
    return pl.pallas_call(
        functools.partial(out_kernel, at),
        grid_spec=pltpu.PrefetchScalarGridSpec(
            num_scalar_prefetch=2,
            grid=(1,),
            in_specs=[whole] * 4,
            out_specs=[whole] * len(result),
            scratch_shapes=[
                pltpu.VMEM((rows, width), jnp.bfloat16),
                pltpu.VMEM((rows, wide), jnp.bfloat16),
                pltpu.VMEM((n, 2, width // 2, TILE), jnp.bfloat16),
                pltpu.VMEM((rows, wide), jnp.bfloat16),
                pltpu.SemaphoreType.DMA((16,)),
                pltpu.SemaphoreType.DMA((1,)),
                pltpu.SemaphoreType.DMA((n, 2)),
                pltpu.SemaphoreType.DMA((n,)),
            ],
        ),
        out_shape=result,
        compiler_params=pltpu.CompilerParams(vmem_limit_bytes=VMEM),
        cost_estimate=COST,
        name="out_project",
    )(phase, retained, mixed, latent, w_mine, w_theirs)


def terms_kernel(half, lengths, mine, theirs, w, out, held, weights, ready, m_sems, w_sems, out_sem):
    rows, depth = mine.shape
    count = lengths.shape[0]
    ends = ends_of(lengths)
    n = weights.shape[0]
    tile = weights.shape[2]

    def m_copy(i, source):
        last = jnp.clip(ends[i] - 1, 0, 2 * rows - 1)
        here = pl.ds(pl.multiple_of(last % rows // 16 * 16, 16), 16)
        return pltpu.make_async_copy(
            source.at[here], held.at[i * 16 : (i + 1) * 16], m_sems.at[i]
        )

    def w_copy(t):
        return pltpu.make_async_copy(
            w.at[:, t * tile : (t + 1) * tile], weights.at[t], w_sems.at[t]
        )

    for i in range(count):
        last = jnp.clip(ends[i] - 1, 0, 2 * rows - 1)

        @pl.when(last // rows == half[0])
        def _():
            m_copy(i, mine).start()

        @pl.when(last // rows != half[0])
        def _():
            m_copy(i, theirs).start()

    for t in range(n):
        w_copy(t).start()
    for i in range(count):
        m_copy(i, mine).wait()
    for t in range(n):
        w_copy(t).wait()
        ready[:, t * tile : (t + 1) * tile] = jnp.dot(
            held[...], weights[t], preferred_element_type=jnp.float32
        ).astype(jnp.bfloat16)
    copy = pltpu.make_async_copy(ready, out, out_sem.at[0])
    copy.start()
    copy.wait()


def score_terms(half, lengths, mine, theirs, w_out):
    depth, width = w_out.shape
    count = lengths.shape[0]
    whole = pl.BlockSpec(memory_space=pltpu.HBM)
    n = 5
    return pl.pallas_call(
        terms_kernel,
        grid_spec=pltpu.PrefetchScalarGridSpec(
            num_scalar_prefetch=2,
            grid=(1,),
            in_specs=[whole] * 3,
            out_specs=whole,
            scratch_shapes=[
                pltpu.VMEM((count * 16, depth), jnp.bfloat16),
                pltpu.VMEM((n, depth, width // n), jnp.bfloat16),
                pltpu.VMEM((count * 16, width), jnp.bfloat16),
                pltpu.SemaphoreType.DMA((count,)),
                pltpu.SemaphoreType.DMA((n,)),
                pltpu.SemaphoreType.DMA((1,)),
            ],
        ),
        out_shape=jax.ShapeDtypeStruct((count * 16, width), jnp.bfloat16),
        compiler_params=pltpu.CompilerParams(vmem_limit_bytes=VMEM),
        cost_estimate=COST,
        name="score_terms",
    )(half, lengths, mine, theirs, w_out)


def score_kernel(half, lengths, rating_ref, mine_ref, theirs_ref, x, out_ref, held, sems):
    rows, width = x.shape
    last = [end - 1 - half[0] * rows for end in ends_of(lengths)]

    def copy(i):
        row = jnp.clip(last[i], 0, rows - 1)
        here = pl.ds(pl.multiple_of(row // 16 * 16, 16), 16)
        return pltpu.make_async_copy(x.at[here], held.at[i], sems.at[i])

    count = held.shape[0]
    for i in range(count):
        copy(i).start()
    out_ref[...] = jnp.zeros_like(out_ref)
    for i in range(count):
        copy(i).wait()
        here = slice(i * 16, (i + 1) * 16)
        summed = held[i].astype(jnp.float32) + (
            mine_ref[here, :].astype(jnp.float32) + theirs_ref[here, :].astype(jnp.float32)
        )
        squares = jnp.sum(summed * summed, axis=-1, keepdims=True) / width
        graded = jnp.sum(summed * rating_ref[...].astype(jnp.float32), axis=-1, keepdims=True)
        graded = graded * lax.rsqrt(squares + epsilon)
        place = lax.broadcasted_iota(jnp.int32, graded.shape, 0)
        wanted = (place == last[i] % 16) & (last[i] >= 0) & (last[i] < rows)
        graded = jnp.sum(jnp.where(wanted, graded, 0.0), axis=0, keepdims=True)
        out_ref[i : i + 1, :] = jnp.broadcast_to(graded, (1, out_ref.shape[1]))


def score(half, lengths, rating, x, mine, theirs):
    width = x.shape[1]
    count = lengths.shape[0]
    spec = pl.BlockSpec(mine.shape, lambda i, h, l: (0, 0))
    return pl.pallas_call(
        score_kernel,
        grid_spec=pltpu.PrefetchScalarGridSpec(
            num_scalar_prefetch=2,
            grid=(1,),
            in_specs=[
                pl.BlockSpec((1, width), lambda i, h, l: (0, 0)),
                spec,
                spec,
                pl.BlockSpec(memory_space=pltpu.HBM),
            ],
            out_specs=pl.BlockSpec((8, 128), lambda i, h, l: (0, 0)),
            scratch_shapes=[
                pltpu.VMEM((count, 16, width), jnp.bfloat16),
                pltpu.SemaphoreType.DMA((count,)),
            ],
        ),
        out_shape=jax.ShapeDtypeStruct((8, 128), jnp.float32),
        compiler_params=pltpu.CompilerParams(vmem_limit_bytes=VMEM),
        cost_estimate=COST,
        name="score",
    )(half, lengths, rating, mine, theirs, x)


def on_device(
    latent_states,
    piece_extents,
    retained_bundles,
    mixer_scaling_factor,
    asker_projector,
    asker_offset_vector,
    lookup_projector,
    content_projector,
    content_offset_vector,
    mixer_output_matrix,
    leave_rating_matrix,
):
    local = latent_states[0, 0, :, 0]
    rows, width = local.shape
    n_dp = lax.axis_size("dp")
    half = lax.axis_index("tensor").astype(jnp.int32).reshape(1)
    phase = lax.axis_index("section").astype(jnp.int32).reshape(1)
    lengths = piece_extents.reshape(piece_extents.shape[-1])
    w_query = asker_projector[0]
    w_key = lookup_projector[0]
    w_value = content_projector[0]
    w_out = mixer_output_matrix[0]
    operands = (
        mixer_scaling_factor,
        asker_offset_vector,
        content_offset_vector,
        w_query,
        w_key,
        w_value,
    )
    q_width = w_query.shape[1]
    k_width = w_key.shape[1]
    forward = [(s, s + 1) for s in range(lax.axis_size("section") - 1)]

    def exchange(value):
        return lax.all_to_all(
            value.reshape(n_dp, rows // n_dp, value.shape[-1]), "dp", 0, 0
        )

    def onward(value):
        return lax.ppermute(value, "section", forward)

    q_width = w_query.shape[1]
    k_width = w_key.shape[1]
    forward = [(s, s + 1) for s in range(lax.axis_size("section") - 1)]

    def exchange(value):
        return lax.all_to_all(
            value.reshape(n_dp, rows // n_dp, value.shape[-1]), "dp", 0, 0
        )

    def onward(value):
        return lax.ppermute(value, "section", forward)

    def after(value, earlier):
        return lax.optimization_barrier((value, earlier))[0]

    other = swap(local)
    latent = exchange(local)
    w_other = swap(after(w_out, other))
    qkv = project_in(half, lengths, local, other, *operands)
    sent = attention(1 - half, lengths, qkv, q_width, k_width)
    received = swap(sent)
    mine = attention(half, lengths, qkv, q_width, k_width)
    mixed = exchange(after(jnp.concatenate([mine, received], axis=1), latent))
    latent = choose(phase, retained_bundles, latent)
    terms = score_terms(half, lengths, mine, sent, w_out)
    mixed = after(mixed, (terms, latent))

    operands = (latent, w_out, w_other)
    first, mixed = out_project(phase, retained_bundles, mixed, *operands, 0, CHUNKS[0])
    (second,) = out_project(phase, retained_bundles, mixed, *operands, *CHUNKS)
    first = onward(first)
    second = exchange(second)
    second, first = lax.optimization_barrier((second, first))
    second = onward(second)
    first = exchange(first)
    arrived = jnp.concatenate([v.reshape(rows, v.shape[-1]) for v in (first, second)], axis=1)

    received = swap(terms)
    scores = score(half, lengths, leave_rating_matrix, local, terms, received)
    seg_scores = lax.psum(scores[: lengths.shape[0], 0], "tensor")
    return (seg_scores[None, None, None], arrived[None, None, :, None, :])


def solution(mesh):
    return jax.shard_map(
        on_device,
        mesh=mesh,
        in_specs=(
            P("section", "dp", "tensor", None, None),
            P("section", "dp", None, None),
            P(),
            P("section", None),
            P("section", None, "tensor"),
            P("section", "tensor"),
            P("section", None, "tensor"),
            P("section", None, "tensor"),
            P("section", "tensor"),
            P("section", "tensor", None),
            P("section", None),
        ),
        out_specs=(P("section", "dp", None, None), P("section", "dp", "tensor", None, None)),
        check_vma=False,
    )
```

time: 179 us -> 166 us (0.927)
  waiting for transfers between devices: 69.3 us -> 35.3 us
  blocking collectives: 2.97 us -> 26.6 us
  Pallas kernels: 67.6 us -> 74.1 us
  other arithmetic: 8.58 us -> 4.34 us
  local copies, waits for them, and re-layouts: 4.24 us -> 0.8 us
  starting transfers between devices: 24.8 us -> 22.8 us
    all_to_all x0 -> x1, blocking collectives: none -> 23.6 us  [exchange(): lax.all_to_all(value.reshape(n_dp, rows // n_dp, value.shape[-1]), 'dp',...]
    ppermute x2, waiting for transfers between devices: 27.4 us -> 4.99 us  [onward(): return lax.ppermute(value, 'section', forward)]
    all_to_all x4 -> x3, waiting for transfers between devices: 41.9 us -> 22.9 us  [exchange(): lax.all_to_all(value.reshape(n_dp, rows // n_dp, value.shape[-1]), 'dp',...]
    ppermute x3 -> x4, waiting for transfers between devices: 0.01 us -> 7.46 us  [swap(): return lax.ppermute(value, 'tensor', [(0, 1), (1, 0)])]
    convert_element_type x2 -> x0, other arithmetic: 6.89 us -> none  [on_device(): outs.append(out.astype(jnp.bfloat16).reshape(n_dp, rows // n_dp, wide))]
    pallas_call x2, Pallas kernels: 28.7 us -> 32.3 us  [the longest x1 21.9 us: project_in(): pl.pallas_call(qkv_kernel, grid_spec=pltpu.PrefetchScalarGridSpec(num_sca...]
    unnamed x8 -> x6, local copies, waits for them, and re-layouts: 3.44 us -> 0.01 us
    pallas_call x1 -> x2, Pallas kernels: 8.3 us -> 11.6 us  [attention(): pl.pallas_call(attention_kernel, grid_spec=pltpu.PrefetchScalarGridSpec(n...]
  transfers between devices with their start and end apart: 9 -> 9, of which waited for: 5 -> 6; matrix products, arithmetic and copies ran while one was open for 4% -> 2% of each run, Pallas kernels for 17% -> 38%
where the time goes in v3:
time: 166 us; the launch traced here: 165 us
  Pallas kernels  74.1 us (45%)
  waiting for transfers between devices  35.3 us (21%)
  blocking collectives  26.6 us (16%)
  starting transfers between devices  22.8 us (14%)
  other arithmetic  4.34 us (3%)
    all_to_all x1, blocking collectives, exchange(): lax.all_to_all(value.reshape(n_dp, rows // n_dp, value.shape[-1]), 'dp',...  23.6 us
    all_to_all x3, waiting for transfers between devices, exchange(): lax.all_to_all(value.reshape(n_dp, rows // n_dp, value.shape[-1]), 'dp',...  22.9 us
    pallas_call x1, Pallas kernels, project_in(): pl.pallas_call(qkv_kernel, grid_spec=pltpu.PrefetchScalarGridSpec(num_sca...  21.9 us
    pallas_call x2, Pallas kernels, out_project(): pl.pallas_call(functools.partial(out_kernel, at), grid_spec=pltpu.Prefetc...  21.6 us
    all_to_all x3, starting transfers between devices, exchange(): lax.all_to_all(value.reshape(n_dp, rows // n_dp, value.shape[-1]), 'dp',...  16.2 us
    pallas_call x2, Pallas kernels, attention(): pl.pallas_call(attention_kernel, grid_spec=pltpu.PrefetchScalarGridSpec(n...  11.6 us
    pallas_call x1, Pallas kernels, score_terms(): pl.pallas_call(terms_kernel, grid_spec=pltpu.PrefetchScalarGridSpec(num_s...  10.4 us
    ppermute x4, waiting for transfers between devices, swap(): return lax.ppermute(value, 'tensor', [(0, 1), (1, 0)])  7.46 us
  transfers between devices with their start and end apart: 9, of which 6 were waited for; matrix products, arithmetic and copies ran while one was open for 2% of the time, Pallas kernels for 38%

profile of v3, /device:TPU:2, one launch (start us, length us, event | category | flops | bytes accessed | tf_op | source)
XLA Modules:
  0.0 164.7 jit_solution(13783525778620877154)
XLA Ops:
  0.6 0.1 collective-permute-start
  0.7 5.2 %collective-permute-done.other = bf16[256,5120]{1,0:T(8,128)(2,1)} collective-permute-done((bf16[256,5120]{1,0:T(8,128)(2,1)}, bf16[256,5120]{1,0:T(8,128)(2,1)}, u32[]{:S(2)}, u32[]{:S(2)}) %collective-permute-start) | collective-permute-done | bytes 2621472 | tf_op jit(solution)/shard_map/ppermute | solution.py:37
  6.0 0.1 collective-permute-start.3
  6.1 8.1 %all-to-all-start = ((bf16[16,16,5120]{2,1,0:T(8,128)(2,1)}), bf16[16,16,5120]{2,1,0:T(8,128)(2,1)S(1)}, u32[]{:S(2)}, u32[]{:S(2)}) async-start(bf16[16,16,5120]{2,1,0:T(8,128)(2,1)} %bitcast.22), calls=%async_computation | async-start | bytes 5242880 | tf_op jit(solution)/shard_map/all_to_all | solution.py:569
  14.2 21.9 %qkv.1.q_ref.k_ref.v_ref = bf16[512,2560]{1,0:T(8,128)(2,1)} custom-call(s32[1]{0:T(128)} %bitcast.half, s32[4]{0:T(128)} %bitcast.33, bf16[1,5120]{1,0:T(2,128)(2,1)} %gain_ref.1, bf16[1,1536]{1,0:T(2,128)(2,1)} %q_bias_ref.1, bf16[1,512]{1,0:T(2,128)(2,1)} %v_bias_ref.1, bf16[256,5120]{1,0:T(8,128)(2,1)} %bitcast.23, ...), custom_call_target="tpu_custom_call" | custom-call | flops 1 | bytes 1 | tf_op jit(solution)/shard_map/qkv/pallas_call | solution.py:137
  36.1 6.7 %attention.3.theirs = bf16[256,1536]{1,0:T(8,128)(2,1)} custom-call(s32[1]{0:T(128)S(6)} %sub.3.half, s32[4]{0:T(128)} %bitcast.34, bf16[512,2560]{1,0:T(8,128)(2,1)} %qkv.1.q_ref.k_ref.v_ref, bf16[512,2560]{1,0:T(8,128)(2,1)} %qkv.1.q_ref.k_ref.v_ref, bf16[512,2560]{1,0:T(8,128)(2,1)} %qkv.1.q_ref.k_ref.v_ref), custom_call_target="tpu_custom_call" | custom-call | flops 1 | bytes 1 | tf_op jit(solution)/shard_map/attention/pallas_call | solution.py:217
  42.8 0.0 collective-permute-start.2
  42.8 4.8 %attention.2.mine = bf16[256,1536]{1,0:T(8,128)(2,1)} custom-call(s32[1]{0:T(128)} %bitcast.half, s32[4]{0:T(128)} %bitcast.35, bf16[512,2560]{1,0:T(8,128)(2,1)} %qkv.1.q_ref.k_ref.v_ref, bf16[512,2560]{1,0:T(8,128)(2,1)} %qkv.1.q_ref.k_ref.v_ref, bf16[512,2560]{1,0:T(8,128)(2,1)} %qkv.1.q_ref.k_ref.v_ref), custom_call_target="tpu_custom_call" | custom-call | flops 1 | bytes 1 | tf_op jit(solution)/shard_map/attention/pallas_call | solution.py:217
  47.7 0.0 collective-permute-done.2
  47.7 2.5 %pad_maximum_fusion = bf16[256,3072]{1,0:T(8,128)(2,1)} fusion(bf16[256,1536]{1,0:T(8,128)(2,1)S(1)} %collective-permute-done.2, bf16[256,1536]{1,0:T(8,128)(2,1)} %attention.2.mine), kind=kLoop, calls=%fused_computation.1 | loop fusion | flops 3145728 | bytes 3145728 | tf_op jit(solution)/shard_map/concatenate | solution.py:586
  50.2 5.2 %all-to-all-done.spread = bf16[16,16,5120]{2,1,0:T(8,128)(2,1)S(1)} async-done(((bf16[16,16,5120]{2,1,0:T(8,128)(2,1)}), bf16[16,16,5120]{2,1,0:T(8,128)(2,1)S(1)}, u32[]{:S(2)}, u32[]{:S(2)}) %all-to-all-start) | async-done | bytes 2621472 | tf_op jit(solution)/shard_map/all_to_all | solution.py:569
  55.3 4.4 %all-to-all-start.1 = ((bf16[16,16,3072]{2,1,0:T(8,128)(2,1)}), bf16[16,16,3072]{2,1,0:T(8,128)(2,1)}, u32[]{:S(2)}, u32[]{:S(2)}) async-start(bf16[16,16,3072]{2,1,0:T(8,128)(2,1)} %bitcast.26), calls=%async_computation.1 | async-start | bytes 3145728 | tf_op jit(solution)/shard_map/all_to_all | solution.py:569
  59.8 0.0 copy-done
  59.8 4.4 %choose.1.latent = bf16[256,5120]{1,0:T(8,128)(2,1)} custom-call(s32[1]{0:T(128)} %bitcast.7.phase, s32[3,16]{1,0:T(4,128)} %retained.5, bf16[16,16,5120]{2,1,0:T(8,128)(2,1)} %copy-done), custom_call_target="tpu_custom_call" | custom-call | flops 1 | bytes 1 | tf_op jit(solution)/shard_map/choose/pallas_call | solution.py:265
  64.2 10.4 %score_terms.1.mine_ref = bf16[64,5120]{1,0:T(8,128)(2,1)} custom-call(s32[1]{0:T(128)} %bitcast.half, s32[4]{0:T(128)} %bitcast.36, bf16[256,1536]{1,0:T(8,128)(2,1)} %attention.2.mine, bf16[256,1536]{1,0:T(8,128)(2,1)} %attention.3.theirs, bf16[1536,5120]{1,0:T(8,128)(2,1)} %bitcast.18), custom_call_target="tpu_custom_call" | custom-call | flops 1 | bytes 1 | tf_op jit(solution)/shard_map/score_terms/pallas_call | solution.py:442
  74.6 10.1 %all-to-all-done.1.mixed = bf16[16,16,3072]{2,1,0:T(8,128)(2,1)} async-done(((bf16[16,16,3072]{2,1,0:T(8,128)(2,1)}), bf16[16,16,3072]{2,1,0:T(8,128)(2,1)}, u32[]{:S(2)}, u32[]{:S(2)}) %all-to-all-start.1) | async-done | bytes 1572896 | tf_op jit(solution)/shard_map/all_to_all | solution.py:569
  84.7 0.0 collective-permute-done.3.w_theirs
  84.7 11.6 %out_project.2 = (bf16[256,2560]{1,0:T(8,128)(2,1)}, bf16[256,3072]{1,0:T(8,128)(2,1)}) custom-call(s32[1]{0:T(128)} %bitcast.7.phase, s32[3,16]{1,0:T(4,128)} %retained.5, bf16[16,16,3072]{2,1,0:T(8,128)(2,1)} %all-to-all-done.1.mixed, bf16[256,5120]{1,0:T(8,128)(2,1)} %choose.1.latent, bf16[1536,5120]{1,0:T(8,128)(2,1)} %bitcast.19, ...), custom_call_target="tpu_custom_call" | custom-call | flops 1 | bytes 1 | tf_op jit(solution)/shard_map/out_project/pallas_call | solution.py:368
  96.3 3.1 %collective-permute-start.4 = (bf16[256,2560]{1,0:T(8,128)(2,1)}, bf16[256,2560]{1,0:T(8,128)(2,1)S(1)}, u32[]{:S(2)}, u32[]{:S(2)}) collective-permute-start(bf16[256,2560]{1,0:T(8,128)(2,1)} %get-tuple-element.13), channel_id=1, source_target_pairs={{0,32},{32,64},{64,96},{1,33},{33,65},{65,97},{2,34},{34,66},{66,9... | collective-permute-start | bytes 3932168 | tf_op jit(solution)/shard_map/ppermute | solution.py:574
  99.4 10.0 %out_project.3 = bf16[256,2560]{1,0:T(8,128)(2,1)} custom-call(s32[1]{0:T(128)} %bitcast.7.phase, s32[3,16]{1,0:T(4,128)} %retained.5, bf16[256,3072]{1,0:T(8,128)(2,1)} %get-tuple-element.12.mixed, bf16[256,5120]{1,0:T(8,128)(2,1)} %choose.1.latent, bf16[1536,5120]{1,0:T(8,128)(2,1)} %bitcast.20, bf16[1536,5120]{1,0:T(8,128)(2,1)} %collective-permute-done.3.w_theirs), custom_call_target="tpu_custom_call" | custom-call | flops 1 | bytes 1 | tf_op jit(solution)/shard_map/out_project/pallas_call | solution.py:368
  109.4 23.6 %all_to_all.20 = bf16[16,16,2560]{2,1,0:T(8,128)(2,1)} all-to-all(bf16[16,16,2560]{2,1,0:T(8,128)(2,1)} %bitcast.27), channel_id=1, replica_groups=mesh['section'=4,'dp'=16,'tensor'=2] {'dp'}, dimensions={0} | all-to-all | bytes 2621440 | tf_op jit(solution)/shard_map/all_to_all | solution.py:569
  133.0 0.0 collective-permute-done.4
  133.0 3.1 %collective-permute-start.5 = (bf16[16,16,2560]{2,1,0:T(8,128)(2,1)}, bf16[16,16,2560]{2,1,0:T(8,128)(2,1)S(1)}, u32[]{:S(2)}, u32[]{:S(2)}) collective-permute-start(bf16[16,16,2560]{2,1,0:T(8,128)(2,1)} %all_to_all.20), channel_id=1, source_target_pairs={{0,32},{32,64},{64,96},{1,33},{33,65},{65,97},{2,34},{34,66},{66,9... | collective-permute-start | bytes 3932168 | tf_op jit(solution)/shard_map/ppermute | solution.py:574
  136.2 3.7 %all-to-all-start.3 = ((bf16[16,16,2560]{2,1,0:T(8,128)(2,1)}), bf16[16,16,2560]{2,1,0:T(8,128)(2,1)S(1)}, u32[]{:S(2)}, u32[]{:S(2)}) async-start(bf16[16,16,2560]{2,1,0:T(8,128)(2,1)} %bitcast.32), calls=%async_computation.3 | async-start | bytes 2621440 | tf_op jit(solution)/shard_map/all_to_all | solution.py:569
  139.9 0.1 collective-permute-start.1
  140.0 2.2 %collective-permute-done.1.theirs_ref = bf16[64,5120]{1,0:T(8,128)(2,1)} collective-permute-done((bf16[64,5120]{1,0:T(8,128)(2,1)S(1)}, bf16[64,5120]{1,0:T(8,128)(2,1)}, u32[]{:S(2)}, u32[]{:S(2)}) %collective-permute-start.1) | collective-permute-done | bytes 655392 | tf_op jit(solution)/shard_map/ppermute | solution.py:37
  142.2 4.3 %score.1 = f32[8,128]{1,0:T(8,128)} custom-call(s32[1]{0:T(128)} %bitcast.half, s32[4]{0:T(128)} %bitcast.37, bf16[1,5120]{1,0:T(2,128)(2,1)} %rating_ref.1, bf16[64,5120]{1,0:T(8,128)(2,1)} %score_terms.1.mine_ref, bf16[64,5120]{1,0:T(8,128)(2,1)} %collective-permute-done.1.theirs_ref, bf16[256,5120]{1,0:T(8,128)(2,1)} %bitcast.24), custom_call_target="tpu_custom_call" | custom-call | flops 1 | bytes 1 | tf_op jit(solution)/shard_map/score/pallas_call | solution.py:497
  146.6 0.8 slice_reduce_fusion
  147.3 3.0 %psum.7 = f32[1,1,1,4]{3,2,1,0:T(1,128)} all-reduce(f32[1,1,1,4]{3,2,1,0:T(1,128)S(1)} %bitcast.38), channel_id=1, replica_groups=mesh['section'=4,'dp'=16,'tensor'=2] {'tensor'}, use_global_device_ids=true, to_apply=%region_0.0 | all-reduce | flops 4 | bytes 32 | tf_op jit(solution)/shard_map/psum | solution.py:603
  150.3 7.6 %all-to-all-done.3 = bf16[16,16,2560]{2,1,0:T(8,128)(2,1)S(1)} async-done(((bf16[16,16,2560]{2,1,0:T(8,128)(2,1)}), bf16[16,16,2560]{2,1,0:T(8,128)(2,1)S(1)}, u32[]{:S(2)}, u32[]{:S(2)}) %all-to-all-start.3) | async-done | bytes 1310752 | tf_op jit(solution)/shard_map/all_to_all | solution.py:569
  157.9 5.0 %collective-permute-done.5 = bf16[16,16,2560]{2,1,0:T(8,128)(2,1)S(1)} collective-permute-done((bf16[16,16,2560]{2,1,0:T(8,128)(2,1)}, bf16[16,16,2560]{2,1,0:T(8,128)(2,1)S(1)}, u32[]{:S(2)}, u32[]{:S(2)}) %collective-permute-start.5) | collective-permute-done | bytes 1310752 | tf_op jit(solution)/shard_map/ppermute | solution.py:574
  162.9 1.8 %maximum_bitcast_fusion = bf16[1,1,256,1,5120]{4,2,3,1,0:T(8,128)(2,1)} fusion(bf16[256,2560]{1,0:T(8,128)(2,1)S(1)} %bitcast.31, bf16[256,2560]{1,0:T(8,128)(2,1)S(1)} %bitcast.28), kind=kLoop, calls=%fused_computation | loop fusion | flops 5242880 | bytes 5242880 | tf_op jit(solution)/shard_map/broadcast_in_dim | solution.py:604
  (5 shorter events, 0.0 us)
Async XLA Ops:
  0.6 5.3 %collective-permute-start = (bf16[256,5120]{1,0:T(8,128)(2,1)}, bf16[256,5120]{1,0:T(8,128)(2,1)}, u32[]{:S(2)}, u32[]{:S(2)}) collective-permute-start(bf16[256,5120]{1,0:T(8,128)(2,1)} %bitcast.21), channel_id=1, source_target_pairs={{0,1},{1,0},{2,3},{3,2},{4,5},{5,4},{6,7},{7,6},{8,9},{9,8},{10,11... | collective-permute-start | bytes 7864328 | tf_op jit(solution)/shard_map/ppermute | solution.py:37
  6.0 78.7 %collective-permute-start.3 = (bf16[1536,5120]{1,0:T(8,128)(2,1)}, bf16[1536,5120]{1,0:T(8,128)(2,1)}, u32[]{:S(2)}, u32[]{:S(2)}) collective-permute-start(bf16[1536,5120]{1,0:T(8,128)(2,1)} %bitcast.17), channel_id=1, source_target_pairs={{0,1},{1,0},{2,3},{3,2},{4,5},{5,4},{6,7},{7,6},{8,9},{9,8},{10,11... | collective-permute-start | bytes 47185928 | tf_op jit(solution)/shard_map/ppermute | solution.py:37
  6.1 49.2 %all-to-all-start = ((bf16[16,16,5120]{2,1,0:T(8,128)(2,1)}), bf16[16,16,5120]{2,1,0:T(8,128)(2,1)S(1)}, u32[]{:S(2)}, u32[]{:S(2)}) async-start(bf16[16,16,5120]{2,1,0:T(8,128)(2,1)} %bitcast.22), calls=%async_computation | async-start | bytes 5242880 | tf_op jit(solution)/shard_map/all_to_all | solution.py:569
  42.8 4.8 %collective-permute-start.2 = (bf16[256,1536]{1,0:T(8,128)(2,1)}, bf16[256,1536]{1,0:T(8,128)(2,1)S(1)}, u32[]{:S(2)}, u32[]{:S(2)}) collective-permute-start(bf16[256,1536]{1,0:T(8,128)(2,1)} %attention.3.theirs), channel_id=1, source_target_pairs={{0,1},{1,0},{2,3},{3,2},{4,5},{5,4},{6,7},{7,6},{8,9},{9,8},{10,11... | collective-permute-start | bytes 2359304 | tf_op jit(solution)/shard_map/ppermute | solution.py:37
  55.3 4.5 %copy-start = (bf16[16,16,5120]{2,1,0:T(8,128)(2,1)}, bf16[16,16,5120]{2,1,0:T(8,128)(2,1)S(1)}, u32[]{:S(2)}) copy-start(bf16[16,16,5120]{2,1,0:T(8,128)(2,1)S(1)} %all-to-all-done.spread) | copy-start | bytes 7864324
  55.3 29.3 %all-to-all-start.1 = ((bf16[16,16,3072]{2,1,0:T(8,128)(2,1)}), bf16[16,16,3072]{2,1,0:T(8,128)(2,1)}, u32[]{:S(2)}, u32[]{:S(2)}) async-start(bf16[16,16,3072]{2,1,0:T(8,128)(2,1)} %bitcast.26), calls=%async_computation.1 | async-start | bytes 3145728 | tf_op jit(solution)/shard_map/all_to_all | solution.py:569
  96.3 36.7 %collective-permute-start.4 = (bf16[256,2560]{1,0:T(8,128)(2,1)}, bf16[256,2560]{1,0:T(8,128)(2,1)S(1)}, u32[]{:S(2)}, u32[]{:S(2)}) collective-permute-start(bf16[256,2560]{1,0:T(8,128)(2,1)} %get-tuple-element.13), channel_id=1, source_target_pairs={{0,32},{32,64},{64,96},{1,33},{33,65},{65,97},{2,34},{34,66},{66,9... | collective-permute-start | bytes 3932168 | tf_op jit(solution)/shard_map/ppermute | solution.py:574
  109.4 30.5 %copy-start.1 = (bf16[64,5120]{1,0:T(8,128)(2,1)S(1)}, bf16[64,5120]{1,0:T(8,128)(2,1)}, u32[]{:S(2)}) copy-start(bf16[64,5120]{1,0:T(8,128)(2,1)} %score_terms.1.mine_ref) | copy-start | bytes 1966084
  133.0 3.1 %copy-start.2 = (bf16[256,2560]{1,0:T(8,128)(2,1)}, bf16[256,2560]{1,0:T(8,128)(2,1)S(1)}, u32[]{:S(2)}) copy-start(bf16[256,2560]{1,0:T(8,128)(2,1)S(1)} %collective-permute-done.4) | copy-start | bytes 3932164
  133.0 29.9 %collective-permute-start.5 = (bf16[16,16,2560]{2,1,0:T(8,128)(2,1)}, bf16[16,16,2560]{2,1,0:T(8,128)(2,1)S(1)}, u32[]{:S(2)}, u32[]{:S(2)}) collective-permute-start(bf16[16,16,2560]{2,1,0:T(8,128)(2,1)} %all_to_all.20), channel_id=1, source_target_pairs={{0,32},{32,64},{64,96},{1,33},{33,65},{65,97},{2,34},{34,66},{66,9... | collective-permute-start | bytes 3932168 | tf_op jit(solution)/shard_map/ppermute | solution.py:574
  136.2 21.7 %all-to-all-start.3 = ((bf16[16,16,2560]{2,1,0:T(8,128)(2,1)}), bf16[16,16,2560]{2,1,0:T(8,128)(2,1)S(1)}, u32[]{:S(2)}, u32[]{:S(2)}) async-start(bf16[16,16,2560]{2,1,0:T(8,128)(2,1)} %bitcast.32), calls=%async_computation.3 | async-start | bytes 2621440 | tf_op jit(solution)/shard_map/all_to_all | solution.py:569
  139.9 2.3 %collective-permute-start.1 = (bf16[64,5120]{1,0:T(8,128)(2,1)S(1)}, bf16[64,5120]{1,0:T(8,128)(2,1)}, u32[]{:S(2)}, u32[]{:S(2)}) collective-permute-start(bf16[64,5120]{1,0:T(8,128)(2,1)S(1)} %copy-done.1), channel_id=1, source_target_pairs={{0,1},{1,0},{2,3},{3,2},{4,5},{5,4},{6,7},{7,6},{8,9},{9,8},{10,11... | collective-permute-start | bytes 1966088 | tf_op jit(solution)/shard_map/ppermute | solution.py:37

commit v4 on v3

--- a/solution.py
+++ b/solution.py
@@ -38,7 +38,7 @@
 
 
 def qkv_kernel(half, lengths, gain_ref, q_bias_ref, v_bias_ref, x, other, wq, wk, wv, *rest):
-    out, held, normed, weights, ready, turns, x_sems, w_sems, out_sems = rest
+    mine, sent, held, normed, weights, ready, turns, passed, x_sems, w_sems, out_sems = rest
     rows, width = normed.shape
     few = rows // 8
     slots, deep = weights.shape[:2]
@@ -63,13 +63,6 @@
             source.at[d * deep : (d + 1) * deep, at : at + TILE],
             weights.at[j % slots],
             w_sems.at[j % slots],
-        )
-
-    def out_copy(t):
-        return pltpu.make_async_copy(
-            ready.at[:, t * TILE : (t + 1) * TILE],
-            out.at[:, t * TILE : (t + 1) * TILE],
-            out_sems.at[t],
         )
 
     for r in range(8):
@@ -122,9 +115,32 @@
                 ready[:, t * TILE + at : t * TILE + at + HD] = turned.astype(jnp.bfloat16)
         else:
             ready[:, here] = part.astype(jnp.bfloat16)
-        out_copy(t).start()
-    for t in range(len(tiles)):
-        out_copy(t).wait()
+
+    q_width, k_width = wq.shape[1], wk.shape[1]
+    ends = ends_of(lengths)
+    q_ref = ready.at[:, :q_width]
+    k_ref = ready.at[:, q_width : q_width + k_width]
+    v_ref = ready.at[:, q_width + k_width :]
+
+    def attend_both(sent_first, mine_first):
+        for i, first in enumerate((sent_first, mine_first)):
+            attend(rows // 2, first, ends, q_ref, k_ref, v_ref, passed.at[i], q_width)
+            out_copy(i).start()
+
+    def out_copy(i):
+        target = (sent, mine.at[:, :q_width])[i]
+        return pltpu.make_async_copy(passed.at[i], target, out_sems.at[i])
+
+    @pl.when(half[0] == 0)
+    def _():
+        attend_both(rows // 2, 0)
+
+    @pl.when(half[0] != 0)
+    def _():
+        attend_both(0, rows // 2)
+
+    for i in range(2):
+        out_copy(i).wait()
 
 
 def project_in(half, lengths, x, other, gain, q_bias, v_bias, wq, wk, wv):
@@ -140,97 +156,64 @@
             num_scalar_prefetch=2,
             grid=(1,),
             in_specs=specs,
-            out_specs=whole,
+            out_specs=[whole, whole],
             scratch_shapes=[
                 pltpu.VMEM((rows, width), jnp.bfloat16),
                 pltpu.VMEM((rows, width), jnp.bfloat16),
                 pltpu.VMEM((AHEAD + 5, width // 5, TILE), jnp.bfloat16),
                 pltpu.VMEM((rows, columns), jnp.bfloat16),
                 pltpu.VMEM((2, rows, HD), jnp.float32),
+                pltpu.VMEM((2, rows // 2, wq.shape[1]), jnp.bfloat16),
                 pltpu.SemaphoreType.DMA((8,)),
                 pltpu.SemaphoreType.DMA((AHEAD + 5,)),
-                pltpu.SemaphoreType.DMA((n,)),
+                pltpu.SemaphoreType.DMA((2,)),
             ],
         ),
-        out_shape=jax.ShapeDtypeStruct((rows, columns), jnp.bfloat16),
+        out_shape=[
+            jax.ShapeDtypeStruct((rows // 2, 2 * wq.shape[1]), jnp.bfloat16),
+            jax.ShapeDtypeStruct((rows // 2, wq.shape[1]), jnp.bfloat16),
+        ],
         compiler_params=pltpu.CompilerParams(vmem_limit_bytes=VMEM),
         cost_estimate=COST,
         name="qkv",
     )(half, lengths, *operands)
 
 
-def attention_kernel(half, lengths, q_ref, k_ref, v_ref, out_ref):
-    ends = ends_of(lengths)
-    rows = q_ref.shape[0]
+def attend(rows, first, ends, q_ref, k_ref, v_ref, out_ref, wide):
     groups = k_ref.shape[1] // HD
-    heads = q_ref.shape[1] // HD // groups
+    heads = wide // HD // groups
     block = 128
-
-    def rows_of(first):
-        for i in range(0, rows, block):
-            hi = first + i + block
-            lo = max(0, hi - 3 * block)
-            here = slice(i, i + block)
-            b = lo + lax.broadcasted_iota(jnp.int32, (hi - lo, block), 0)
-            a = hi - block + lax.broadcasted_iota(jnp.int32, (hi - lo, block), 1)
-            start = starts_at(hi - block + lax.broadcasted_iota(jnp.int32, (1, block), 1), ends)
-            allowed = (b <= a) & (b >= start)
-            allowed = jnp.concatenate([allowed] * heads, axis=1)
-            for g in range(groups):
-                at = slice(g * HD, (g + 1) * HD)
-                places = [slice(h * HD, (h + 1) * HD) for h in range(g * heads, (g + 1) * heads)]
-                q = jnp.concatenate([q_ref[here, place] for place in places], axis=0)
-                logits = lax.dot_general(
-                    k_ref[lo:hi, at],
-                    q,
-                    (((1,), (1,)), ((), ())),
-                    preferred_element_type=jnp.float32,
-                ) * HD ** (-0.5)
-                logits = jnp.where(allowed, logits, -1e30)
-                expons = jnp.exp(logits - jnp.max(logits, axis=0, keepdims=True))
-                probs = expons * (1.0 / jnp.sum(expons, axis=0, keepdims=True))
-                mixed = lax.dot_general(
-                    probs.astype(jnp.bfloat16),
-                    v_ref[lo:hi, at],
-                    (((0,), (0,)), ((), ())),
-                    preferred_element_type=jnp.float32,
-                ).astype(jnp.bfloat16)
-                for h, place in enumerate(places):
-                    out_ref[here, place] = mixed[h * block : (h + 1) * block]
-
-    @pl.when(half[0] == 0)
-    def _():
-        rows_of(0)
-
-    @pl.when(half[0] != 0)
-    def _():
-        rows_of(rows)
-
-
-def attention(half, lengths, qkv, q_width, k_width):
-    length = qkv.shape[0]
-    rows = length // 2
-    pace = 2
-    steps = k_width // HD // pace
-    wide = q_width // steps
-    deep = k_width // steps
-    return pl.pallas_call(
-        attention_kernel,
-        grid_spec=pltpu.PrefetchScalarGridSpec(
-            num_scalar_prefetch=2,
-            grid=(steps,),
-            in_specs=[
-                pl.BlockSpec((rows, wide), lambda g, h, l: (h[0], g)),
-                pl.BlockSpec((length, deep), lambda g, h, l: (0, q_width // deep + g)),
-                pl.BlockSpec((length, deep), lambda g, h, l: (0, (q_width + k_width) // deep + g)),
-            ],
-            out_specs=pl.BlockSpec((rows, wide), lambda g, h, l: (0, g)),
-        ),
-        out_shape=jax.ShapeDtypeStruct((rows, q_width), jnp.bfloat16),
-        compiler_params=pltpu.CompilerParams(vmem_limit_bytes=VMEM),
-        cost_estimate=COST,
-        name="attention",
-    )(half, lengths, qkv, qkv, qkv)
+    for i in range(0, rows, block):
+        hi = first + i + block
+        lo = max(0, hi - 3 * block)
+        here = slice(i, i + block)
+        there = slice(hi - block, hi)
+        b = lo + lax.broadcasted_iota(jnp.int32, (hi - lo, block), 0)
+        a = hi - block + lax.broadcasted_iota(jnp.int32, (hi - lo, block), 1)
+        start = starts_at(hi - block + lax.broadcasted_iota(jnp.int32, (1, block), 1), ends)
+        allowed = (b <= a) & (b >= start)
+        allowed = jnp.concatenate([allowed] * heads, axis=1)
+        for g in range(groups):
+            at = slice(g * HD, (g + 1) * HD)
+            places = [slice(h * HD, (h + 1) * HD) for h in range(g * heads, (g + 1) * heads)]
+            q = jnp.concatenate([q_ref[there, place] for place in places], axis=0)
+            logits = lax.dot_general(
+                k_ref[lo:hi, at],
+                q,
+                (((1,), (1,)), ((), ())),
+                preferred_element_type=jnp.float32,
+            ) * HD ** (-0.5)
+            logits = jnp.where(allowed, logits, -1e30)
+            expons = jnp.exp(logits - jnp.max(logits, axis=0, keepdims=True))
+            probs = expons * (1.0 / jnp.sum(expons, axis=0, keepdims=True))
+            mixed = lax.dot_general(
+                probs.astype(jnp.bfloat16),
+                v_ref[lo:hi, at],
+                (((0,), (0,)), ((), ())),
+                preferred_element_type=jnp.float32,
+            ).astype(jnp.bfloat16)
+            for h, place in enumerate(places):
+                out_ref[here, place] = mixed[h * block : (h + 1) * block]
 
 
 def choose_kernel(phase, retained, spread, chosen, held, in_sems, out_sems):
@@ -309,10 +292,10 @@
             source = mixed.at[jnp.clip(wanted[k], 0, packs - 1)]
             return pltpu.make_async_copy(source, held.at[k * few : (k + 1) * few], m_sems.at[k])
 
+        for k in range(packs):
+            m_copy(k).start()
         for copy in w_copies(0):
             copy.start()
-        for k in range(packs):
-            m_copy(k).start()
         l_copy.start()
         for k in range(packs):
             m_copy(k).wait()
@@ -333,14 +316,13 @@
     for copy in w_copies(1):
         copy.start()
     for t in range(n):
-        for copy in w_copies(t):
-            copy.wait()
         if t + 2 < n:
             for copy in w_copies(t + 2):
                 copy.start()
         here = slice(t * TILE, (t + 1) * TILE)
         branch = 0.0
         for i in range(2):
+            w_copies(t)[i].wait()
             term = jnp.dot(
                 held[:, i * depth : (i + 1) * depth],
                 weights[t, i],
@@ -391,7 +373,7 @@
 
 
 def terms_kernel(half, lengths, mine, theirs, w, out, held, weights, ready, m_sems, w_sems, out_sem):
-    rows, depth = mine.shape
+    rows, depth = theirs.shape
     count = lengths.shape[0]
     ends = ends_of(lengths)
     n = weights.shape[0]
@@ -401,7 +383,7 @@
         last = jnp.clip(ends[i] - 1, 0, 2 * rows - 1)
         here = pl.ds(pl.multiple_of(last % rows // 16 * 16, 16), 16)
         return pltpu.make_async_copy(
-            source.at[here], held.at[i * 16 : (i + 1) * 16], m_sems.at[i]
+            source.at[here, :depth], held.at[i * 16 : (i + 1) * 16], m_sems.at[i]
         )
 
     def w_copy(t):
@@ -549,8 +531,6 @@
         w_key,
         w_value,
     )
-    q_width = w_query.shape[1]
-    k_width = w_key.shape[1]
     forward = [(s, s + 1) for s in range(lax.axis_size("section") - 1)]
 
     def exchange(value):
@@ -561,8 +541,6 @@
     def onward(value):
         return lax.ppermute(value, "section", forward)
 
-    q_width = w_query.shape[1]
-    k_width = w_key.shape[1]
     forward = [(s, s + 1) for s in range(lax.axis_size("section") - 1)]
 
     def exchange(value):
@@ -578,12 +556,11 @@
 
     other = swap(local)
     latent = exchange(local)
-    w_other = swap(after(w_out, other))
-    qkv = project_in(half, lengths, local, other, *operands)
-    sent = attention(1 - half, lengths, qkv, q_width, k_width)
+    mine, sent = project_in(half, lengths, local, other, *operands)
     received = swap(sent)
-    mine = attention(half, lengths, qkv, q_width, k_width)
-    mixed = exchange(after(jnp.concatenate([mine, received], axis=1), latent))
+    mine = lax.dynamic_update_slice(mine, after(received, latent), (0, received.shape[1]))
+    w_other = swap(after(w_out, mine))
+    mixed = exchange(mine)
     latent = choose(phase, retained_bundles, latent)
     terms = score_terms(half, lengths, mine, sent, w_out)
     mixed = after(mixed, (terms, latent))
@@ -593,14 +570,15 @@
     (second,) = out_project(phase, retained_bundles, mixed, *operands, *CHUNKS)
     first = onward(first)
     second = exchange(second)
-    second, first = lax.optimization_barrier((second, first))
+    theirs = swap(terms)
+    scores = score(half, lengths, leave_rating_matrix, local, terms, theirs)
+    seg_scores = lax.psum(scores[: lengths.shape[0], 0], "tensor")
+    second, first, seg_scores = lax.optimization_barrier((second, first, seg_scores))
+    first = exchange(first)
     second = onward(second)
-    first = exchange(first)
-    arrived = jnp.concatenate([v.reshape(rows, v.shape[-1]) for v in (first, second)], axis=1)
-
-    received = swap(terms)
-    scores = score(half, lengths, leave_rating_matrix, local, terms, received)
-    seg_scores = lax.psum(scores[: lengths.shape[0], 0], "tensor")
+    first = lax.pad(first.reshape(rows, CHUNKS[0]), jnp.bfloat16(0), ((0, 0, 0), (0, CHUNKS[1], 0)))
+    arrived = lax.dynamic_update_slice(first, second.reshape(rows, CHUNKS[1]), (0, CHUNKS[0]))
+
     return (seg_scores[None, None, None], arrived[None, None, :, None, :])
 
 

time: 166 us -> 165 us (level)
  waiting for transfers between devices: 35.3 us -> 42.8 us
  Pallas kernels: 74.1 us -> 68.2 us
  other arithmetic: 4.34 us -> 1.83 us
    all_to_all x3, waiting for transfers between devices: 22.9 us -> 36.5 us  [exchange(): lax.all_to_all(value.reshape(n_dp, rows // n_dp, value.shape[-1]), 'dp',...]
    pallas_call x2 -> x0, Pallas kernels: 11.6 us -> none  [attention(): pl.pallas_call(attention_kernel, grid_spec=pltpu.PrefetchScalarGridSpec(n...]
    pallas_call x1, Pallas kernels: 21.9 us -> 27.5 us  [project_in(): pl.pallas_call(qkv_kernel, grid_spec=pltpu.PrefetchScalarGridSpec(num_sca...]
    ppermute x4, waiting for transfers between devices: 7.46 us -> 2.22 us  [swap(): return lax.ppermute(value, 'tensor', [(0, 1), (1, 0)])]
    concatenate x1 -> x0, other arithmetic: 2.5 us -> none  [on_device(): mixed = exchange(after(jnp.concatenate([mine, received], axis=1), latent))]
  transfers between devices with their start and end apart: 9 -> 9, of which waited for: 6 -> 5; matrix products, arithmetic and copies ran while one was open for 2% -> 0% of each run, Pallas kernels for 38% -> 35%
where the time goes in v4:
time: 165 us; the launch traced here: 164 us
  Pallas kernels  68.2 us (41%)
  waiting for transfers between devices  42.8 us (26%)
  blocking collectives  25.8 us (16%)
  starting transfers between devices  23 us (14%)
  local copies, waits for them, and re-layouts  1.89 us (1%)
  other arithmetic  1.83 us (1%)
    all_to_all x3, waiting for transfers between devices, exchange(): lax.all_to_all(value.reshape(n_dp, rows // n_dp, value.shape[-1]), 'dp',...  36.5 us
    pallas_call x1, Pallas kernels, project_in(): pl.pallas_call(qkv_kernel, grid_spec=pltpu.PrefetchScalarGridSpec(num_sca...  27.5 us
    all_to_all x1, blocking collectives, exchange(): lax.all_to_all(value.reshape(n_dp, rows // n_dp, value.shape[-1]), 'dp',...  22.9 us
    pallas_call x2, Pallas kernels, out_project(): pl.pallas_call(functools.partial(out_kernel, at), grid_spec=pltpu.Prefetc...  21.3 us
    all_to_all x3, starting transfers between devices, exchange(): lax.all_to_all(value.reshape(n_dp, rows // n_dp, value.shape[-1]), 'dp',...  16.3 us
    pallas_call x1, Pallas kernels, score_terms(): pl.pallas_call(terms_kernel, grid_spec=pltpu.PrefetchScalarGridSpec(num_s...  10.4 us
    ppermute x2, starting transfers between devices, onward(): return lax.ppermute(value, 'section', forward)  6.31 us
    pallas_call x1, Pallas kernels, choose(): pl.pallas_call(choose_kernel, grid_spec=pltpu.PrefetchScalarGridSpec(num_...  4.71 us
  transfers between devices with their start and end apart: 9, of which 5 were waited for; matrix products, arithmetic and copies ran while one was open for 0% of the time, Pallas kernels for 35%

profile of v4, /device:TPU:2, one launch (start us, length us, event | category | flops | bytes accessed | tf_op | source)
XLA Modules:
  0.0 164.4 jit_solution(9948894591341744716)
XLA Ops:
  0.6 0.1 collective-permute-start
  0.7 8.1 %all-to-all-start = ((bf16[16,16,5120]{2,1,0:T(8,128)(2,1)}), bf16[16,16,5120]{2,1,0:T(8,128)(2,1)S(1)}, u32[]{:S(2)}, u32[]{:S(2)}) async-start(bf16[16,16,5120]{2,1,0:T(8,128)(2,1)} %bitcast.22), calls=%async_computation | async-start | bytes 5242880 | tf_op jit(solution)/shard_map/all_to_all | solution.py:547
  8.8 0.0 collective-permute-done.other
  8.8 27.5 %qkv.1 = (bf16[256,3072]{1,0:T(8,128)(2,1)}, bf16[256,1536]{1,0:T(8,128)(2,1)}) custom-call(s32[1]{0:T(128)} %bitcast.1.half, s32[4]{0:T(128)} %bitcast.33, bf16[1,5120]{1,0:T(2,128)(2,1)} %gain_ref.1, bf16[1,1536]{1,0:T(2,128)(2,1)} %q_bias_ref.1, bf16[1,512]{1,0:T(2,128)(2,1)} %v_bias_ref.1, bf16[256,5120]{1,0:T(8,128)(2,1)} %bitcast.23, ...), custom_call_target="tpu_custom_call" | custom-call | flops 1 | bytes 1 | tf_op jit(solution)/shard_map/qkv/pallas_call | solution.py:153
  36.3 0.2 collective-permute-start.1
  36.5 13.9 %all-to-all-done.spread = bf16[16,16,5120]{2,1,0:T(8,128)(2,1)S(1)} async-done(((bf16[16,16,5120]{2,1,0:T(8,128)(2,1)}), bf16[16,16,5120]{2,1,0:T(8,128)(2,1)S(1)}, u32[]{:S(2)}, u32[]{:S(2)}) %all-to-all-start) | async-done | bytes 2621472 | tf_op jit(solution)/shard_map/all_to_all | solution.py:547
  50.4 0.0 collective-permute-done.1
  50.4 1.1 constant_dynamic-update-slice_fusion.mine
  51.5 0.0 collective-permute-start.2
  51.5 4.4 %all-to-all-start.1 = ((bf16[16,16,3072]{2,1,0:T(8,128)(2,1)}), bf16[16,16,3072]{2,1,0:T(8,128)(2,1)}, u32[]{:S(2)}, u32[]{:S(2)}) async-start(bf16[16,16,3072]{2,1,0:T(8,128)(2,1)} %bitcast.26), calls=%async_computation.1 | async-start | bytes 3145728 | tf_op jit(solution)/shard_map/all_to_all | solution.py:547
  55.9 0.0 copy-done
  55.9 4.7 %choose.1.latent = bf16[256,5120]{1,0:T(8,128)(2,1)} custom-call(s32[1]{0:T(128)} %bitcast.phase, s32[3,16]{1,0:T(4,128)} %retained.5, bf16[16,16,5120]{2,1,0:T(8,128)(2,1)} %copy-done), custom_call_target="tpu_custom_call" | custom-call | flops 1 | bytes 1 | tf_op jit(solution)/shard_map/choose/pallas_call | solution.py:248
  60.6 10.4 %score_terms.1.mine_ref = bf16[64,5120]{1,0:T(8,128)(2,1)} custom-call(s32[1]{0:T(128)} %bitcast.1.half, s32[4]{0:T(128)} %bitcast.34, bf16[256,3072]{1,0:T(8,128)(2,1)} %constant_dynamic-update-slice_fusion.mine, bf16[256,1536]{1,0:T(8,128)(2,1)} %get-tuple-element.13.theirs, bf16[1536,5120]{1,0:T(8,128)(2,1)} %bitcast.18), custom_call_target="tpu_custom_call" | custom-call | flops 1 | bytes 1 | tf_op jit(solution)/shard_map/score_terms/pallas_call | solution.py:424
  71.0 12.4 %all-to-all-done.1.mixed = bf16[16,16,3072]{2,1,0:T(8,128)(2,1)} async-done(((bf16[16,16,3072]{2,1,0:T(8,128)(2,1)}), bf16[16,16,3072]{2,1,0:T(8,128)(2,1)}, u32[]{:S(2)}, u32[]{:S(2)}) %all-to-all-start.1) | async-done | bytes 1572896 | tf_op jit(solution)/shard_map/all_to_all | solution.py:547
  83.4 0.0 collective-permute-done.2.w_theirs
  83.4 11.4 %out_project.2 = (bf16[256,2560]{1,0:T(8,128)(2,1)}, bf16[256,3072]{1,0:T(8,128)(2,1)}) custom-call(s32[1]{0:T(128)} %bitcast.phase, s32[3,16]{1,0:T(4,128)} %retained.5, bf16[16,16,3072]{2,1,0:T(8,128)(2,1)} %all-to-all-done.1.mixed, bf16[256,5120]{1,0:T(8,128)(2,1)} %choose.1.latent, bf16[1536,5120]{1,0:T(8,128)(2,1)} %bitcast.19, ...), custom_call_target="tpu_custom_call" | custom-call | flops 1 | bytes 1 | tf_op jit(solution)/shard_map/out_project/pallas_call | solution.py:350
  94.8 3.2 %collective-permute-start.3 = (bf16[256,2560]{1,0:T(8,128)(2,1)}, bf16[256,2560]{1,0:T(8,128)(2,1)S(1)}, u32[]{:S(2)}, u32[]{:S(2)}) collective-permute-start(bf16[256,2560]{1,0:T(8,128)(2,1)} %get-tuple-element.18), channel_id=1, source_target_pairs={{0,32},{32,64},{64,96},{1,33},{33,65},{65,97},{2,34},{34,66},{66,9... | collective-permute-start | bytes 3932168 | tf_op jit(solution)/shard_map/ppermute | solution.py:552
  98.1 9.9 %out_project.3 = bf16[256,2560]{1,0:T(8,128)(2,1)} custom-call(s32[1]{0:T(128)} %bitcast.phase, s32[3,16]{1,0:T(4,128)} %retained.5, bf16[256,3072]{1,0:T(8,128)(2,1)} %get-tuple-element.17.mixed, bf16[256,5120]{1,0:T(8,128)(2,1)} %choose.1.latent, bf16[1536,5120]{1,0:T(8,128)(2,1)} %bitcast.20, bf16[1536,5120]{1,0:T(8,128)(2,1)} %collective-permute-done.2.w_theirs), custom_call_target="tpu_custom_call" | custom-call | flops 1 | bytes 1 | tf_op jit(solution)/shard_map/out_project/pallas_call | solution.py:350
  108.0 0.0 copy-start.1
  108.0 3.8 %all-to-all-start.2 = ((bf16[16,16,2560]{2,1,0:T(8,128)(2,1)}), bf16[16,16,2560]{2,1,0:T(8,128)(2,1)S(1)}, u32[]{:S(2)}, u32[]{:S(2)}) async-start(bf16[16,16,2560]{2,1,0:T(8,128)(2,1)} %bitcast.27), calls=%async_computation.2 | async-start | bytes 2621440 | tf_op jit(solution)/shard_map/all_to_all | solution.py:547
  111.9 0.0 copy-done.1
  111.9 0.1 collective-permute-start.4
  112.0 2.2 %collective-permute-done.4.theirs_ref = bf16[64,5120]{1,0:T(8,128)(2,1)} collective-permute-done((bf16[64,5120]{1,0:T(8,128)(2,1)S(1)}, bf16[64,5120]{1,0:T(8,128)(2,1)}, u32[]{:S(2)}, u32[]{:S(2)}) %collective-permute-start.4) | collective-permute-done | bytes 655392 | tf_op jit(solution)/shard_map/ppermute | solution.py:37
  114.2 4.3 %score.1 = f32[8,128]{1,0:T(8,128)} custom-call(s32[1]{0:T(128)} %bitcast.1.half, s32[4]{0:T(128)} %bitcast.35, bf16[1,5120]{1,0:T(2,128)(2,1)} %rating_ref.1, bf16[64,5120]{1,0:T(8,128)(2,1)} %score_terms.1.mine_ref, bf16[64,5120]{1,0:T(8,128)(2,1)} %collective-permute-done.4.theirs_ref, bf16[256,5120]{1,0:T(8,128)(2,1)} %bitcast.24), custom_call_target="tpu_custom_call" | custom-call | flops 1 | bytes 1 | tf_op jit(solution)/shard_map/score/pallas_call | solution.py:479
  118.5 0.8 slice_reduce_fusion
  119.3 3.0 %psum.7 = f32[4]{0:T(128)} all-reduce(f32[4]{0:T(128)S(1)} %slice_reduce_fusion), channel_id=1, replica_groups=mesh['section'=4,'dp'=16,'tensor'=2] {'tensor'}, use_global_device_ids=true, to_apply=%region_0.0 | all-reduce | flops 4 | bytes 32 | tf_op jit(solution)/shard_map/psum | solution.py:575
  122.3 10.2 %all-to-all-done.2 = bf16[16,16,2560]{2,1,0:T(8,128)(2,1)S(1)} async-done(((bf16[16,16,2560]{2,1,0:T(8,128)(2,1)}), bf16[16,16,2560]{2,1,0:T(8,128)(2,1)S(1)}, u32[]{:S(2)}, u32[]{:S(2)}) %all-to-all-start.2) | async-done | bytes 1310752 | tf_op jit(solution)/shard_map/all_to_all | solution.py:547
  132.5 0.0 collective-permute-done.3
  132.5 3.1 %collective-permute-start.5 = (bf16[16,16,2560]{2,1,0:T(8,128)(2,1)S(1)}, bf16[16,16,2560]{2,1,0:T(8,128)(2,1)S(1)}, u32[]{:S(2)}, u32[]{:S(2)}) collective-permute-start(bf16[16,16,2560]{2,1,0:T(8,128)(2,1)S(1)} %all-to-all-done.2), channel_id=1, source_target_pairs={{0,32},{32,64},{64,96},{1,33},{33,65},{65,97},{2,34},{34,66},{66,9... | collective-permute-start | bytes 3932168 | tf_op jit(solution)/shard_map/ppermute | solution.py:552
  135.6 22.9 %all_to_all.20 = bf16[16,16,2560]{2,1,0:T(8,128)(2,1)S(1)} all-to-all(bf16[16,16,2560]{2,1,0:T(8,128)(2,1)S(1)} %bitcast.32), channel_id=1, replica_groups=mesh['section'=4,'dp'=16,'tensor'=2] {'dp'}, dimensions={0} | all-to-all | bytes 2621440 | tf_op jit(solution)/shard_map/all_to_all | solution.py:547
  158.5 4.0 %collective-permute-done.5 = bf16[16,16,2560]{2,1,0:T(8,128)(2,1)S(1)} collective-permute-done((bf16[16,16,2560]{2,1,0:T(8,128)(2,1)S(1)}, bf16[16,16,2560]{2,1,0:T(8,128)(2,1)S(1)}, u32[]{:S(2)}, u32[]{:S(2)}) %collective-permute-start.5) | collective-permute-done | bytes 1310752 | tf_op jit(solution)/shard_map/ppermute | solution.py:552
  162.5 1.8 %maximum_bitcast_fusion = bf16[1,1,256,1,5120]{4,2,3,1,0:T(8,128)(2,1)} fusion(bf16[256,2560]{1,0:T(8,128)(2,1)S(1)} %bitcast.31, bf16[256,2560]{1,0:T(8,128)(2,1)S(1)} %bitcast.30), kind=kLoop, calls=%fused_computation | loop fusion | flops 5242880 | bytes 5242880 | tf_op jit(solution)/shard_map/broadcast_in_dim | solution.py:582
  (1 shorter events, 0.0 us)
Async XLA Ops:
  0.6 8.2 %collective-permute-start = (bf16[256,5120]{1,0:T(8,128)(2,1)}, bf16[256,5120]{1,0:T(8,128)(2,1)}, u32[]{:S(2)}, u32[]{:S(2)}) collective-permute-start(bf16[256,5120]{1,0:T(8,128)(2,1)} %bitcast.21), channel_id=1, source_target_pairs={{0,1},{1,0},{2,3},{3,2},{4,5},{5,4},{6,7},{7,6},{8,9},{9,8},{10,11... | collective-permute-start | bytes 7864328 | tf_op jit(solution)/shard_map/ppermute | solution.py:37
  0.7 49.7 %all-to-all-start = ((bf16[16,16,5120]{2,1,0:T(8,128)(2,1)}), bf16[16,16,5120]{2,1,0:T(8,128)(2,1)S(1)}, u32[]{:S(2)}, u32[]{:S(2)}) async-start(bf16[16,16,5120]{2,1,0:T(8,128)(2,1)} %bitcast.22), calls=%async_computation | async-start | bytes 5242880 | tf_op jit(solution)/shard_map/all_to_all | solution.py:547
  36.3 14.1 %collective-permute-start.1 = (bf16[256,1536]{1,0:T(8,128)(2,1)}, bf16[256,1536]{1,0:T(8,128)(2,1)S(1)}, u32[]{:S(2)}, u32[]{:S(2)}) collective-permute-start(bf16[256,1536]{1,0:T(8,128)(2,1)} %get-tuple-element.13.theirs), channel_id=1, source_target_pairs={{0,1},{1,0},{2,3},{3,2},{4,5},{5,4},{6,7},{7,6},{8,9},{9,8},{10,11... | collective-permute-start | bytes 2359304 | tf_op jit(solution)/shard_map/ppermute | solution.py:37
  50.4 5.5 %copy-start = (bf16[16,16,5120]{2,1,0:T(8,128)(2,1)}, bf16[16,16,5120]{2,1,0:T(8,128)(2,1)S(1)}, u32[]{:S(2)}) copy-start(bf16[16,16,5120]{2,1,0:T(8,128)(2,1)S(1)} %all-to-all-done.spread) | copy-start | bytes 7864324
  51.5 32.0 %collective-permute-start.2 = (bf16[1536,5120]{1,0:T(8,128)(2,1)}, bf16[1536,5120]{1,0:T(8,128)(2,1)}, u32[]{:S(2)}, u32[]{:S(2)}) collective-permute-start(bf16[1536,5120]{1,0:T(8,128)(2,1)} %bitcast.17), channel_id=1, source_target_pairs={{0,1},{1,0},{2,3},{3,2},{4,5},{5,4},{6,7},{7,6},{8,9},{9,8},{10,11... | collective-permute-start | bytes 47185928 | tf_op jit(solution)/shard_map/ppermute | solution.py:37
  51.5 32.0 %all-to-all-start.1 = ((bf16[16,16,3072]{2,1,0:T(8,128)(2,1)}), bf16[16,16,3072]{2,1,0:T(8,128)(2,1)}, u32[]{:S(2)}, u32[]{:S(2)}) async-start(bf16[16,16,3072]{2,1,0:T(8,128)(2,1)} %bitcast.26), calls=%async_computation.1 | async-start | bytes 3145728 | tf_op jit(solution)/shard_map/all_to_all | solution.py:547
  94.8 37.7 %collective-permute-start.3 = (bf16[256,2560]{1,0:T(8,128)(2,1)}, bf16[256,2560]{1,0:T(8,128)(2,1)S(1)}, u32[]{:S(2)}, u32[]{:S(2)}) collective-permute-start(bf16[256,2560]{1,0:T(8,128)(2,1)} %get-tuple-element.18), channel_id=1, source_target_pairs={{0,32},{32,64},{64,96},{1,33},{33,65},{65,97},{2,34},{34,66},{66,9... | collective-permute-start | bytes 3932168 | tf_op jit(solution)/shard_map/ppermute | solution.py:552
  108.0 3.9 %copy-start.1 = (bf16[64,5120]{1,0:T(8,128)(2,1)S(1)}, bf16[64,5120]{1,0:T(8,128)(2,1)}, u32[]{:S(2)}) copy-start(bf16[64,5120]{1,0:T(8,128)(2,1)} %score_terms.1.mine_ref) | copy-start | bytes 1966084
  108.0 24.5 %all-to-all-start.2 = ((bf16[16,16,2560]{2,1,0:T(8,128)(2,1)}), bf16[16,16,2560]{2,1,0:T(8,128)(2,1)S(1)}, u32[]{:S(2)}, u32[]{:S(2)}) async-start(bf16[16,16,2560]{2,1,0:T(8,128)(2,1)} %bitcast.27), calls=%async_computation.2 | async-start | bytes 2621440 | tf_op jit(solution)/shard_map/all_to_all | solution.py:547
  111.9 2.3 %collective-permute-start.4 = (bf16[64,5120]{1,0:T(8,128)(2,1)S(1)}, bf16[64,5120]{1,0:T(8,128)(2,1)}, u32[]{:S(2)}, u32[]{:S(2)}) collective-permute-start(bf16[64,5120]{1,0:T(8,128)(2,1)S(1)} %copy-done.1), channel_id=1, source_target_pairs={{0,1},{1,0},{2,3},{3,2},{4,5},{5,4},{6,7},{7,6},{8,9},{9,8},{10,11... | collective-permute-start | bytes 1966088 | tf_op jit(solution)/shard_map/ppermute | solution.py:37
  132.5 30.0 %collective-permute-start.5 = (bf16[16,16,2560]{2,1,0:T(8,128)(2,1)S(1)}, bf16[16,16,2560]{2,1,0:T(8,128)(2,1)S(1)}, u32[]{:S(2)}, u32[]{:S(2)}) collective-permute-start(bf16[16,16,2560]{2,1,0:T(8,128)(2,1)S(1)} %all-to-all-done.2), channel_id=1, source_target_pairs={{0,32},{32,64},{64,96},{1,33},{33,65},{65,97},{2,34},{34,66},{66,9... | collective-permute-start | bytes 3932168 | tf_op jit(solution)/shard_map/ppermute | solution.py:552
